TPU v7x, 32 devices: a whole 2x2x4 slice. The times are simulated.
32 devices in a mesh: gx: 4 (over y, core), gy: 8 (over z, x).
Axes of the slice: x: 2, y: 2, z: 4, core: 2. Of those that a mesh axis runs over, the one named last changes fastest.
Arguments:
- displacement: float32 [3, 96, 64, 128], P(None, 'gx', 'gy'), may hold values from -6 to 6
- velocity: float32 [3, 96, 64, 128], P(None, 'gx', 'gy'), may hold values from -6 to 6
- external_force: float32 [3, 96, 64, 128], P(None, 'gx', 'gy'), may hold values from -6 to 6
- node_mass: float32 [96, 64, 128], P('gx', 'gy'), may hold values from 0.5 to 2
- stiffness: float32 [96, 64, 128], P('gx', 'gy'), may hold values from 0.5 to 2
- cloak_list: int32 [4, 8, 48], P('gx'), may hold values from -1 to 191, as said below
- micro_state: float32 [4, 8, 128, 48, 128], P('gx', 'gy'), may hold values from -6 to 6
- localization: float32 [256, 6], replicated, may hold values from -3.6 to 3.6
- modes: float32 [256, 128], replicated, may hold values from -0.5 to 0.5
- point_weight: float32 [256], replicated, may hold values from 0.5 to 2
- point_modulus: float32 [256], replicated, may hold values from 1 to 10
- softening: float32 [256], replicated, may hold values from 0.2 to 2
Outputs:
- displacement_next: float32 [3, 96, 64, 128], P(None, 'gx', 'gy')
- velocity_next: float32 [3, 96, 64, 128], P(None, 'gx', 'gy')
- micro_state_next: float32 [4, 8, 128, 48, 128], P('gx', 'gy')
Inputs may be any that keep to these rules, and one draw needn't show every extreme that they name: cloak_list[p, t, :] holds distinct pencil indices x * 8 + y of tile (p, t) in ascending order followed by -1; in every gx index exactly one tile lists 48 pencils and every other tile lists between 20 and 24 pencils, 20 reached in every gx index; the tiles sharing a gx index list exactly 192 pencils together.
All inputs are finite; a program needn't handle non-finite values.
Results may differ from a plain program's by a relative error of at most 0.0003.
Values sent between devices are 32-bit elements; how exact they have to be, the bound alone decides.
No kernel may reach another device: no remote copies, remote signals or barrier semaphores. Data moves between devices by JAX's collectives and lax.ppermute only.
A program may use at most 64 MiB of HBM per device.

v0:
```python
import functools

import jax
import jax.numpy as jnp
from jax import lax
from jax.experimental import pallas as pl
from jax.experimental.pallas import tpu as pltpu
from jax.sharding import PartitionSpec as P

ITERS = 3
STEP = 0.25
HIGHEST = lax.Precision.HIGHEST
F32 = jnp.float32
BF16 = jnp.bfloat16
GRANT = 60 * 2**20
VMEM = pl.BlockSpec(memory_space=pltpu.VMEM)
HBM = pl.BlockSpec(memory_space=pltpu.HBM)
SMEM = pl.BlockSpec(memory_space=pltpu.SMEM)


def split(x):
    high = x.astype(BF16)
    return high, (x - high.astype(F32)).astype(BF16)


def dot(a, b):
    return jnp.dot(a, b, preferred_element_type=F32)


def exact(a, b):
    return jnp.dot(a, b, precision=HIGHEST, preferred_element_type=F32)


def transposed_product(a, b):
    terms = []
    for x in (a, b):
        one = x.astype(BF16).astype(F32)
        two = (x - one).astype(BF16).astype(F32)
        terms.append((one, two, x - one - two))
    (a1, a2, a3), (b1, b2, b3) = terms
    left = jnp.concatenate([a1, a1, a2, a2, a1, a3], axis=0).astype(BF16)
    right = jnp.concatenate([b1, b2, b1, b2, b3, b1], axis=0).astype(BF16)
    return lax.dot_general(left, right, (((0,), (0,)), ((), ())), preferred_element_type=F32)


def lane_of(x, k):
    return jnp.take_along_axis(x, jnp.full(x.shape, k, jnp.int32), axis=1, mode="promise_in_bounds")


def row_of(x, s):
    return jnp.take_along_axis(x, jnp.full(x.shape, s, jnp.int32), axis=0, mode="promise_in_bounds")


def invert_two(a, b, c):
    scale = 1.0 / (a * c - b * b)
    return c * scale, -(b * scale), a * scale


def inverse(matrix):
    size = matrix.shape[0]
    tile = (8, size)
    count = size // 8
    blocks = [matrix[i : i + 8] for i in range(0, size, 8)]
    lane = lax.broadcasted_iota(jnp.int32, tile, 1)
    row = lax.broadcasted_iota(jnp.int32, tile, 0)

    def spread(x, s):
        return jnp.broadcast_to(x[s : s + 1, :], tile)

    for b in range(count):
        before = panel = blocks[b]
        for s in range(0, 8, 4):
            k = b * 8 + s
            lanes4 = jnp.logical_and(lane >= k, lane < k + 4)
            rows4 = jnp.logical_and(row >= s, row < s + 4)
            c = [lane_of(panel, k + i) for i in range(4)]
            r = [
                jnp.where(lane == k + i, 1.0, jnp.where(lanes4, 0.0, spread(panel, s + i)))
                for i in range(4)
            ]
            p = [[row_of(c[j], s + i) for j in range(i + 1)] for i in range(4)]
            (b00, b01), (b10, b11) = p[2][:2], p[3][:2]
            i00, i10, i11 = invert_two(p[0][0], p[1][0], p[1][1])
            w00, w01 = b00 * i00 + b01 * i10, b00 * i10 + b01 * i11
            w10, w11 = b10 * i00 + b11 * i10, b10 * i10 + b11 * i11
            j00, j10, j11 = invert_two(
                p[2][2] - (w00 * b00 + w01 * b01),
                p[3][2] - (w10 * b00 + w11 * b01),
                p[3][3] - (w10 * b10 + w11 * b11),
            )
            y2 = r[2] - (w00 * r[0] + w01 * r[1])
            y3 = r[3] - (w10 * r[0] + w11 * r[1])
            n2, n3 = j00 * y2 + j10 * y3, j10 * y2 + j11 * y3
            n0 = (i00 * r[0] + i10 * r[1]) - (w00 * n2 + w10 * n3)
            n1 = (i10 * r[0] + i11 * r[1]) - (w01 * n2 + w11 * n3)
            f = [jnp.where(row == s + i, -1.0, jnp.where(rows4, 0.0, c[i])) for i in range(4)]
            rest = jnp.where(jnp.logical_or(lanes4, rows4), 0.0, panel)
            panel = rest - ((f[0] * n0 + f[1] * n1) + (f[2] * n2 + f[3] * n3))
        inside = jnp.logical_and(lane >= b * 8, lane < b * 8 + 8)
        panel = jnp.where(inside, -panel, panel)
        change = transposed_product(before, panel)
        for i in range(count):
            old = blocks[i]
            kept = jnp.where(inside, 0.0, old)
            if i == b:
                blocks[i] = panel
            elif i == b + 1:
                t = [lane_of(old, b * 8 + s) * spread(panel, s) for s in range(8)]
                blocks[i] = kept - (((t[0] + t[1]) + (t[2] + t[3])) + ((t[4] + t[5]) + (t[6] + t[7])))
            else:
                blocks[i] = kept - change[i * 8 : i * 8 + 8]
    return -jnp.concatenate(blocks, axis=0)


def near(a, b):
    (ah, al), (bh, bl) = split(a), split(b)
    return dot(ah, bh) + dot(al, bh) + dot(ah, bl)


def fetch(sources, targets, sems):
    copies = [
        pltpu.make_async_copy(a, b, sems.at[i]) for i, (a, b) in enumerate(zip(sources, targets))
    ]
    for copy in copies:
        copy.start()
    for copy in copies:
        copy.wait()


def order_entries(rows, columns, lists_ref, order_ref):
    member = lax.axis_index("gy")
    most = lists_ref.shape[1]
    pencils = [lists_ref[member, e] for e in range(most)]
    listed = [(p >= 0).astype(jnp.int32) for p in pencils]
    edge = [
        jnp.logical_or(p >= (rows - 1) * columns, lax.rem(p, columns) == columns - 1).astype(jnp.int32)
        for p in pencils
    ]
    edges, number = sum(edge), sum(listed)
    next_edge, next_inner, next_rest = 0, edges, number
    for e in range(most):
        inner = listed[e] - edge[e]
        place = jnp.where(edge[e] > 0, next_edge, jnp.where(inner > 0, next_inner, next_rest))
        order_ref[0, place] = e
        order_ref[1, place] = pencils[e]
        next_edge = next_edge + edge[e]
        next_inner = next_inner + inner
        next_rest = next_rest + (1 - listed[e])
    order_ref[0, most] = edges
    order_ref[0, most + 1] = number


def matrices_kernel(
    rows, columns,
    modes_hbm, local_hbm, weight_hbm, modulus_hbm, soft_hbm, lists_ref,
    start0_ref, start1_ref, high_ref, low_ref, back_ref, stress_ref, order_ref,
    wide, modes_ref, local_ref, weight_ref, modulus_ref, soft_ref, sems,
):
    fetch(
        (modes_hbm, local_hbm, weight_hbm, modulus_hbm, soft_hbm),
        (modes_ref, local_ref, weight_ref, modulus_ref, soft_ref),
        sems,
    )
    points, count = modes_ref.shape
    order_entries(rows, columns, lists_ref, order_ref)
    modes = modes_ref[...]
    modes_t = modes.T
    weight = weight_ref[...] / points
    modulus = modulus_ref[...]
    root = jnp.sqrt(soft_ref[...])
    scale = weight * modulus / root
    inverted = inverse(exact(modes_t * (weight * modulus), modes))
    wide[...] = jnp.zeros_like(wide)
    wide[0 : local_ref.shape[0], :] = local_ref[...]
    local = wide[...]
    stress_ref[...] = (local * scale).astype(BF16)
    high, low = split(modes_t * root)
    start0_ref[0:count] = high
    start0_ref[count:] = high
    start1_ref[0:count] = low
    soft_local = local[0:8] * root
    local_high = soft_local.astype(BF16).astype(F32)
    part = [local_high, local_high, soft_local - local_high, jnp.zeros_like(local_high)]
    start1_ref[count:] = jnp.concatenate(part * (count // 32), axis=0).astype(BF16)
    back = near((modes_t * scale).T, inverted)
    high, low = split(back)
    back_ref[:, 0:count] = high
    back_ref[:, count:] = low
    newton = near(back, modes_t * root)
    high, low = split(newton)
    high_ref[...] = high
    low_ref[...] = low


def respond(u):
    return u * lax.rsqrt(1.0 + u * u)


def cells(states, strains, start0, start1, newton_high, newton_low, back, stress_m):
    layers = states[0].shape[1]
    count = states[0].shape[0]
    number = len(states)
    part = min(2, number)
    turned = [state.T for state in states]
    place = lax.broadcasted_iota(jnp.int32, (layers, count), 1) // 32
    strain_parts = []
    each = count // 32
    for q in range(0, number, each):
        rows = []
        for strain in strains[q : q + each]:
            high = strain.astype(BF16).astype(F32)
            rows += [high, strain - high, high, jnp.zeros_like(high)]
        rows = jnp.concatenate(rows, axis=0).T
        strain_parts += [jnp.where(place == g, rows, 0.0).astype(BF16) for g in range(each)]
    start = []
    for c in range(0, number, part):
        high, low = split(jnp.concatenate(turned[c : c + part], axis=0))
        strain = jnp.concatenate(strain_parts[c : c + part], axis=0)
        start.append(
            dot(jnp.concatenate([high, low], axis=1), start0)
            + dot(jnp.concatenate([high, strain], axis=1), start1)
        )
    now = start
    for step in range(ITERS - 1):
        later = []
        for u in now:
            high, low = split(respond(u))
            later.append(u - (dot(high, newton_high) + dot(low, newton_high) + dot(high, newton_low)))
        now = later
    last, moved = [], []
    for first, u in zip(start, now):
        h = respond(u)
        last.append(u - dot(h.astype(BF16), newton_high))
        moved.append(split(first - u + h))
    new_states, stresses = [], []
    for c, (high, low) in enumerate(moved):
        both = dot(high, back)
        change = both[:, 0:count] + both[:, count:] + dot(low, back[:, 0:count])
        for g in range(part):
            new_states.append(states[c * part + g] - change[g * layers : (g + 1) * layers].T)
    for u in last:
        stress = lax.dot_general(
            stress_m, respond(u).astype(BF16), (((1,), (1,)), ((), ())), preferred_element_type=F32
        )
        stresses += [stress[0:8, g * layers : (g + 1) * layers] for g in range(part)]
    return new_states, stresses


def set_pencil(ref, entry, value):
    groups, count, group, layers = ref.shape
    place = lax.div(entry, group) * (count * group) + lax.rem(entry, group)
    ref.reshape(groups * count * group, layers)[pl.ds(place, count, stride=group), :] = value


def run_group(base, group, order_ref, state_ref, strain_ref, weights, stress_s, spare):
    count = weights[4].shape[1] // 2
    most = state_ref.shape[0] // count
    entries = [order_ref[0, base + g] for g in range(group)]
    pencils = [order_ref[1, base + g] for g in range(group)]
    states = [state_ref[pl.ds(e, count, stride=most), :] for e in entries]
    strains = [
        strain_ref[pl.ds(pl.multiple_of(jnp.maximum(p, 0) * 8, 8), 8), :] for p in pencils
    ]
    new_states, stresses = cells(states, strains, *(w[...] for w in weights))
    for g in range(group):
        spot = jnp.where(pencils[g] >= 0, pencils[g], spare)
        stress_s[pl.ds(pl.multiple_of(spot * 8, 8), 8), :] = stresses[g]
    return entries, [jnp.where(p >= 0, a, 0.0) for p, a in zip(pencils, new_states)]


def fluxes(s, side_mean, side_diff):
    lane_zero = lax.broadcasted_iota(jnp.int32, s[0].shape, 1) == 0

    def along(v):
        down = jnp.where(lane_zero, 0.0, pltpu.roll(v, 1, 1))
        return 0.5 * (v + down), v - down

    first = [along(side_mean(s[c]))[0] for c in (0, 5, 4)]
    second = [along(side_diff(s[c]))[0] for c in (5, 1, 3)]
    third = [along(side_mean(s[c]))[1] for c in (4, 3, 2)]
    half = [0.5 * (second[c] + third[c]) for c in range(3)]
    return [(first[c] + half[c], half[c] - first[c]) for c in range(3)]


def row_fluxes(stress_ref, i, columns):
    s = [stress_ref[pl.ds(i * columns * 8 + c, columns, stride=8), :] for c in range(6)]
    first_sub = lax.broadcasted_iota(jnp.int32, s[0].shape, 0) == 0

    def shift(v):
        return jnp.where(first_sub, 0.0, pltpu.roll(v, 1, 0))

    return fluxes(s, lambda v: 0.5 * (v + shift(v)), lambda v: v - shift(v))


def first_groups(order_ref, most, group):
    return lax.div(order_ref[0, most] + (group - 1), group)


def edges_kernel(disp_hbm, xface_ref, yface_ref, corner_ref, disp_ref, sems):
    fetch((disp_hbm,), (disp_ref,), sems)
    for c in range(3):
        xface_ref[c] = disp_ref[c, 0]
        yface_ref[c] = disp_ref[c, :, 0, :]
        corner_ref[c : c + 1] = disp_ref[c, 0, 0:1]


def edge_kernel(
    group, order_ref, disp_ref, xhalo_ref, yhalo_ref, corner_ref, stiff_ref, state_ref,
    start0_ref, start1_ref, high_ref, low_ref, back_ref, stress_ref,
    xface_ref, yface_ref, cface_ref, strain_ref, stress_out, done_ref,
):
    rows, columns, layers = stiff_ref.shape
    most = order_ref.shape[1] - 2
    count = state_ref.shape[0] // most
    weights = (start0_ref, start1_ref, high_ref, low_ref, back_ref, stress_ref)
    tile = (columns, layers)
    lane = lax.broadcasted_iota(jnp.int32, tile, 1)
    sub = lax.broadcasted_iota(jnp.int32, tile, 0)
    last_lane = lane == layers - 1
    last_sub = sub == columns - 1

    def node_row(c, i):
        own = disp_ref[c, i] if i < rows else xhalo_ref[c]
        edge = yhalo_ref[c, i : i + 1] if i < rows else corner_ref[c : c + 1]
        up = jnp.where(last_sub, jnp.broadcast_to(edge, tile), pltpu.roll(own, columns - 1, 0))
        mean, diff = 0.5 * (up + own), up - own
        mean_up = jnp.where(last_lane, 0.0, pltpu.roll(mean, layers - 1, 1))
        diff_up = jnp.where(last_lane, 0.0, pltpu.roll(diff, layers - 1, 1))
        return 0.5 * (mean_up + mean), 0.5 * (diff_up + diff), mean_up - mean

    lower = [node_row(c, 0) for c in range(3)]
    zero_tile = jnp.zeros(tile, F32)
    for i in range(rows):
        upper = [node_row(c, i + 1) for c in range(3)]
        g = [
            (upper[c][0] - lower[c][0], 0.5 * (upper[c][1] + lower[c][1]), 0.5 * (upper[c][2] + lower[c][2]))
            for c in range(3)
        ]
        lower = upper
        strain = [g[0][0], g[1][1], g[2][2], g[1][2] + g[2][1], g[0][2] + g[2][0], g[0][1] + g[1][0]]
        stiffness = stiff_ref[i]
        volume = strain[0] + strain[1] + strain[2]
        for c in range(8):
            place = pl.ds(i * columns * 8 + c, columns, stride=8)
            if c >= 6:
                strain_ref[place, :] = zero_tile
                continue
            strain_ref[place, :] = strain[c]
            stress_out[place, :] = stiffness * (volume + 2.0 * strain[c] if c < 3 else strain[c])

    def body(q, carry):
        _, states = run_group(
            q * group, group, order_ref, state_ref, strain_ref, weights, stress_out, rows * columns
        )
        for g in range(group):
            done_ref[pl.ds(pl.multiple_of((q * group + g) * count, count), count), :] = states[g]
        return carry

    lax.fori_loop(0, first_groups(order_ref, most, group), body, 0)

    last = row_fluxes(stress_out, rows - 1, columns)
    for c in range(3):
        xface_ref[c] = -last[c][1]
    s = [stress_out[pl.ds((columns - 1) * 8 + c, rows, stride=columns * 8), :] for c in range(6)]
    side = fluxes(s, lambda v: 0.5 * v, lambda v: -v)
    for c in range(3):
        yface_ref[c] = -side[c][0]
        yface_ref[c, 1:rows] = yface_ref[c, 1:rows] - side[c][1][0 : rows - 1]
        cface_ref[c : c + 1] = -side[c][1][rows - 1 : rows]


def inner_kernel(
    rows, columns, order_ref, state_ref, strain_ref, stress_in, done_ref,
    start0_ref, start1_ref, high_ref, low_ref, back_ref, stress_ref,
    force_ref, out_hbm,
    stress_s, out_s, sems,
):
    groups, count, group, layers = out_s.shape
    most = groups * group
    weights = (start0_ref, start1_ref, high_ref, low_ref, back_ref, stress_ref)
    before = first_groups(order_ref, most, group)
    after = lax.div(order_ref[0, most + 1] + (group - 1), group)
    stress_s[...] = stress_in[...]

    def store(q):
        return pltpu.make_async_copy(
            out_s.at[q], out_hbm.at[:, pl.ds(q * group, group), :], sems.at[q]
        )

    def copy(q, carry):
        for g in range(group):
            place = q * group + g
            set_pencil(
                out_s, order_ref[0, place],
                done_ref[pl.ds(pl.multiple_of(place * count, count), count), :],
            )
        return carry

    def clear(q, carry):
        for g in range(group):
            set_pencil(out_s, order_ref[0, q * group + g], jnp.zeros((count, layers), F32))
        return carry

    lax.fori_loop(0, before, copy, 0)
    lax.fori_loop(jnp.maximum(before, after), groups, clear, 0)

    def body(q, sent):
        entries, states = run_group(
            q * group, group, order_ref, state_ref, strain_ref, weights, stress_s, rows * columns
        )
        for g in range(group):
            set_pencil(out_s, entries[g], states[g])
        whole = jnp.maximum(sent, lax.div(entries[group - 1] + 1, group))

        def send(chunk, carry):
            store(chunk).start()
            return carry

        lax.fori_loop(sent, whole, send, 0)
        return whole

    sent = lax.fori_loop(before, after, body, 0)

    def send(chunk, carry):
        store(chunk).start()
        return carry

    lax.fori_loop(sent, groups, send, 0)

    below = None
    for i in range(rows):
        here = row_fluxes(stress_s, i, columns)
        for c in range(3):
            force_ref[c, i] = -here[c][0] if below is None else -(here[c][0] + below[c][1])
        below = here
    for q in range(groups):
        store(q).wait()


def update_kernel(
    disp_ref, velocity_ref, external_ref, mass_ref, force_ref, xface_ref, yface_ref, cface_ref,
    disp_out, velocity_out,
):
    rows, columns, layers = mass_ref.shape
    first_sub = lax.broadcasted_iota(jnp.int32, (columns, layers), 0) == 0
    for i in range(rows):
        factor = STEP / mass_ref[i]
        for c in range(3):
            edge = yface_ref[c, i : i + 1]
            if i == 0:
                edge = edge + cface_ref[c : c + 1]
            internal = force_ref[c, i] + jnp.where(
                first_sub, jnp.broadcast_to(edge, (columns, layers)), 0.0
            )
            if i == 0:
                internal = internal + xface_ref[c]
            velocity = velocity_ref[c, i] + factor * (external_ref[c, i] - internal)
            velocity_out[c, i] = velocity
            disp_out[c, i] = disp_ref[c, i] + STEP * velocity


def shape(*dims, dtype=F32):
    return jax.ShapeDtypeStruct(dims, dtype)


def on_device(
    displacement, velocity, external_force, node_mass, stiffness, cloak_list, micro_state,
    localization, modes, point_weight, point_modulus, softening,
):
    rows, columns, layers = stiffness.shape
    points, count = modes.shape
    most = cloak_list.shape[2]
    gx, gy = lax.axis_size("gx"), lax.axis_size("gy")
    along_x = [(i + 1, i) for i in range(gx - 1)]
    along_y = [(i + 1, i) for i in range(gy - 1)]
    both = [((i + 1) * gy + j + 1, i * gy + j) for i in range(gx - 1) for j in range(gy - 1)]
    back = lambda pairs: [(b, a) for a, b in pairs]
    group = 8
    xhalo, yhalo, corner = pl.pallas_call(
        edges_kernel,
        out_shape=(shape(3, columns, layers), shape(3, rows, layers), shape(3, layers)),
        in_specs=[HBM],
        out_specs=(VMEM,) * 3,
        scratch_shapes=[pltpu.VMEM(displacement.shape, F32), pltpu.SemaphoreType.DMA((1,))],
        compiler_params=pltpu.CompilerParams(vmem_limit_bytes=GRANT),
        cost_estimate=pl.CostEstimate(flops=10**10, bytes_accessed=10**6, transcendentals=0),
    )(displacement)
    xhalo = lax.ppermute(xhalo, "gx", along_x)
    yhalo = lax.ppermute(yhalo, "gy", along_y)
    corner = lax.ppermute(corner, ("gx", "gy"), both)

    *matrices, order = pl.pallas_call(
        functools.partial(matrices_kernel, rows, columns),
        out_shape=tuple(shape(n, points, dtype=BF16) for n in (2 * count, 2 * count, points, points))
        + (
            shape(points, 2 * count, dtype=BF16), shape(16, points, dtype=BF16),
            shape(2, most + 2, dtype=jnp.int32),
        ),
        in_specs=[HBM] * 5 + [SMEM],
        out_specs=(VMEM,) * 6 + (SMEM,),
        scratch_shapes=[
            pltpu.VMEM((16, points), F32), pltpu.VMEM((points, count), F32),
            pltpu.VMEM((localization.shape[1], points), F32),
        ]
        + [pltpu.VMEM((1, points), F32)] * 3
        + [pltpu.SemaphoreType.DMA((5,))],
        compiler_params=pltpu.CompilerParams(vmem_limit_bytes=16 * 2**20),
        cost_estimate=pl.CostEstimate(flops=10**10, bytes_accessed=10**6, transcendentals=0),
    )(
        modes, localization.T, point_weight.reshape(1, points), point_modulus.reshape(1, points),
        softening.reshape(1, points), cloak_list[0],
    )

    groups = most // group
    states = micro_state.reshape(count * most, layers)
    strain_shape = shape(rows * columns * 8, layers)
    stress_shape = shape(rows * columns * 8 + 8, layers)
    xface, yface, cface, strain, stress, done = pl.pallas_call(
        functools.partial(edge_kernel, group),
        out_shape=(
            shape(3, columns, layers), shape(3, rows, layers), shape(3, layers),
            strain_shape, stress_shape, shape(most * count, layers),
        ),
        in_specs=[SMEM] + [VMEM] * 12,
        out_specs=(VMEM,) * 6,
        compiler_params=pltpu.CompilerParams(vmem_limit_bytes=30 * 2**20),
        cost_estimate=pl.CostEstimate(flops=10**10, bytes_accessed=10**7, transcendentals=0),
    )(order, displacement, xhalo, yhalo, corner, stiffness, states, *matrices)

    xface = lax.ppermute(xface, "gx", back(along_x))
    yface = lax.ppermute(yface, "gy", back(along_y))
    cface = lax.ppermute(cface, ("gx", "gy"), back(both))

    force, new_state = pl.pallas_call(
        functools.partial(inner_kernel, rows, columns),
        out_shape=(shape(3, rows, columns, layers), shape(count, most, layers)),
        in_specs=[SMEM] + [VMEM] * 10,
        out_specs=(VMEM, HBM),
        scratch_shapes=[
            pltpu.VMEM(stress_shape.shape, F32), pltpu.VMEM((groups, count, group, layers), F32),
            pltpu.SemaphoreType.DMA((groups,)),
        ],
        compiler_params=pltpu.CompilerParams(vmem_limit_bytes=30 * 2**20),
        cost_estimate=pl.CostEstimate(flops=2 * 10**10, bytes_accessed=10**7, transcendentals=0),
    )(order, states, strain, stress, done, *matrices)

    displacement_next, velocity_next = pl.pallas_call(
        update_kernel,
        out_shape=(shape(3, rows, columns, layers),) * 2,
        in_specs=[VMEM] * 8,
        out_specs=(VMEM,) * 2,
        compiler_params=pltpu.CompilerParams(vmem_limit_bytes=16 * 2**20),
    )(displacement, velocity, external_force, node_mass, force, xface, yface, cface)
    return displacement_next, velocity_next, new_state.reshape(micro_state.shape)


def solution(mesh):
    field = P(None, "gx", "gy", None)
    grid = P("gx", "gy", None)
    state = P("gx", "gy", None, None, None)
    in_specs = (field, field, field, grid, grid, P("gx", None, None), state, P(), P(), P(), P(), P())
    return jax.shard_map(
        on_device, mesh=mesh, in_specs=in_specs, out_specs=(field, field, state), check_vma=False
    )
```

profile of v0, /device:TPU:16, one launch (start us, length us, event | category | flops | bytes accessed | tf_op | source)
XLA Modules:
  0.0 43.4 jit_solution(12879038352369555562)
XLA Ops:
  0.6 0.0 copy-start.11
  0.6 0.0 copy-start.10
  0.7 0.0 copy-start.9
  0.7 0.0 copy-start.5
  0.7 0.0 copy-start.7
  0.7 0.0 copy-start.8
  0.7 1.7 %shard_map.140 = (f32[3,8,128]{2,1,0:T(8,128)}, f32[3,24,128]{2,1,0:T(8,128)}, f32[3,128]{1,0:T(4,128)}) custom-call(f32[3,24,8,128]{3,2,1,0:T(8,128)} %disp_ref.3), custom_call_target="tpu_custom_call" | custom-call | flops 10000000000 | bytes 1000000 | tf_op jit(solution)/shard_map/pallas_call | solution.py:479
  2.4 1.3 %collective-permute-start.2 = (f32[3,128]{1,0:T(4,128)}, f32[3,128]{1,0:T(4,128)S(1)}, u32[]{:S(2)}, u32[]{:S(2)}) collective-permute-start(f32[3,128]{1,0:T(4,128)} %get-tuple-element.26), channel_id=1, source_target_pairs={{9,0},{10,1},{11,2},{12,3},{13,4},{14,5},{15,6},{17,8},{18,9},{19,... | collective-permute-start | bytes 4616 | tf_op jit(solution)/shard_map/ppermute | solution.py:490
  3.7 1.3 %collective-permute-start = (f32[3,8,128]{2,1,0:T(8,128)}, f32[3,8,128]{2,1,0:T(8,128)S(1)}, u32[]{:S(2)}, u32[]{:S(2)}) collective-permute-start(f32[3,8,128]{2,1,0:T(8,128)} %get-tuple-element.24), channel_id=1, source_target_pairs={{8,0},{16,8},{24,16},{9,1},{17,9},{25,17},{10,2},{18,10},{26,18},{... | collective-permute-start | bytes 36872 | tf_op jit(solution)/shard_map/ppermute | solution.py:488
  5.0 3.3 %collective-permute-start.1 = (f32[3,24,128]{2,1,0:T(8,128)}, f32[3,24,128]{2,1,0:T(8,128)S(1)}, u32[]{:S(2)}, u32[]{:S(2)}) collective-permute-start(f32[3,24,128]{2,1,0:T(8,128)} %get-tuple-element.25), channel_id=1, source_target_pairs={{1,0},{2,1},{3,2},{4,3},{5,4},{6,5},{7,6},{9,8},{10,9},{11,10},{12... | collective-permute-start | bytes 110600 | tf_op jit(solution)/shard_map/ppermute | solution.py:489
  8.3 0.0 copy-done.11
  8.3 0.0 copy-done.10
  8.3 0.0 copy-done.9
  8.3 0.0 copy-done.5
  8.3 0.0 copy-done.7
  8.3 0.0 copy-done.8
  8.3 0.0 copy-start
  8.4 0.0 copy-start.4
  8.4 0.0 copy-start.6
  8.4 6.3 %shard_map.139 = (bf16[256,256]{1,0:T(8,128)(2,1)S(1)}, bf16[256,256]{1,0:T(8,128)(2,1)S(1)}, bf16[256,256]{1,0:T(8,128)(2,1)S(1)}, bf16[256,256]{1,0:T(8,128)(2...) custom-call(f32[256,128]{1,0:T(8,128)S(1)} %copy-done.5, ...), custom_call_target="tpu_custom_call" | custom-call | flops 10000000000 | bytes 1000000 | tf_op jit(solution)/shard_map/pallas_call | solution.py:492
  14.7 0.0 collective-permute-done.2.corner_ref
  14.7 0.0 collective-permute-done.xhalo_ref
  14.7 0.0 collective-permute-done.1.yhalo_ref
  14.7 0.0 copy-done
  14.8 0.0 copy-done.4
  14.8 0.0 copy-done.6
  14.8 3.2 %shard_map.141 = (f32[3,8,128]{2,1,0:T(8,128)S(1)}, f32[3,24,128]{2,1,0:T(8,128)S(1)}, f32[3,128]{1,0:T(4,128)S(1)}, f32[1536,128]{1,0:T(8,128)S(1)}, f32[1544,128]{1,0:T(8,128)S(1)}, /*index=5*/f32[6144,128]{1,0:T(8,128)S(1)}) custom-call(s32[2,50]{1,0:T(2,128)S(1)} %get-tuple-element.23.order_ref, f32[3,24,8,128]{3,2,1,0:T(8,128)S(1)} %copy-done, ...), custom_call_target="tpu_custom_call" | custom-call | flops 10000000000 | bytes 10000000 | tf_op jit(solution)/shard_map/pallas_call | solution.py:518
  18.0 4.6 %collective-permute-start.5 = (f32[3,128]{1,0:T(4,128)S(1)}, f32[3,128]{1,0:T(4,128)S(1)}, u32[]{:S(2)}, u32[]{:S(2)}) collective-permute-start(f32[3,128]{1,0:T(4,128)S(1)} %get-tuple-element.39), channel_id=1, source_target_pairs={{0,9},{1,10},{2,11},{3,12},{4,13},{5,14},{6,15},{8,17},{9,18},{10,... | collective-permute-start | bytes 4616 | tf_op jit(solution)/shard_map/ppermute | solution.py:532
  22.6 1.6 %collective-permute-start.3 = (f32[3,8,128]{2,1,0:T(8,128)S(1)}, f32[3,8,128]{2,1,0:T(8,128)S(1)}, u32[]{:S(2)}, u32[]{:S(2)}) collective-permute-start(f32[3,8,128]{2,1,0:T(8,128)S(1)} %get-tuple-element.37), channel_id=1, source_target_pairs={{0,8},{8,16},{16,24},{1,9},{9,17},{17,25},{2,10},{10,18},{18,26},{... | collective-permute-start | bytes 36872 | tf_op jit(solution)/shard_map/ppermute | solution.py:530
  24.3 5.6 %collective-permute-start.4 = (f32[3,24,128]{2,1,0:T(8,128)S(1)}, f32[3,24,128]{2,1,0:T(8,128)S(1)}, u32[]{:S(2)}, u32[]{:S(2)}) collective-permute-start(f32[3,24,128]{2,1,0:T(8,128)S(1)} %get-tuple-element.38), channel_id=1, source_target_pairs={{0,1},{1,2},{2,3},{3,4},{4,5},{5,6},{6,7},{8,9},{9,10},{10,11},{11... | collective-permute-start | bytes 110600 | tf_op jit(solution)/shard_map/ppermute | solution.py:531
  29.9 0.0 copy-start.1
  29.9 0.0 copy-start.2
  29.9 0.0 copy-start.3
  29.9 12.5 %shard_map.142 = (f32[3,24,8,128]{3,2,1,0:T(8,128)S(1)}, f32[128,48,128]{2,1,0:T(8,128)}) custom-call(s32[2,50]{1,0:T(2,128)S(1)} %get-tuple-element.23.order_ref, f32[6144,128]{1,0:T(8,128)S(1)} %bitcast.8, f32[1536,128]{1,0:T(8,128)S(1)} %get-tuple-element.33.strain_ref, f32[1544,128]{1,0:T(8,128)S(1)} %get-tuple-element.34.stress_in, ...), custom_call_target="tpu_custom_call" | custom-call | flops 20000000000 | bytes 10000000 | tf_op jit(solution)/shard_map/pallas_call | solution.py:534
  42.4 0.0 collective-permute-done.5.cface_ref
  42.4 0.0 collective-permute-done.3.xface_ref
  42.4 0.0 collective-permute-done.4.yface_ref
  42.4 0.0 copy-done.1
  42.5 0.0 copy-done.2
  42.5 0.0 copy-done.3
  42.5 0.9 %shard_map.143 = (f32[3,24,8,128]{3,2,1,0:T(8,128)}, f32[3,24,8,128]{3,2,1,0:T(8,128)}) custom-call(f32[3,24,8,128]{3,2,1,0:T(8,128)S(1)} %copy-done, f32[3,24,8,128]{3,2,1,0:T(8,128)S(1)} %copy-done.1, f32[3,24,8,128]{3,2,1,0:T(8,128)S(1)} %copy-done.2, f32[24,8,128]{2,1,0:T(8,128)S(1)} %copy-done.3, f32[3,24,8,128]{3,2,1,0:T(8,128)S(1)} %get-tuple-element.36.force_ref, ...), custom_call_target="tpu_custom_call" | custom-call | tf_op jit(solution)/shard_map/pallas_call | solution.py:547
Async XLA Ops:
  0.6 7.7 %copy-start.11 = (f32[256]{0:T(256)S(1)}, f32[256]{0:T(256)}, u32[]{:S(2)}) copy-start(f32[256]{0:T(256)} %param.23) | copy-start | bytes 3076
  0.6 7.7 %copy-start.10 = (f32[256]{0:T(256)S(1)}, f32[256]{0:T(256)}, u32[]{:S(2)}) copy-start(f32[256]{0:T(256)} %param.22) | copy-start | bytes 3076
  0.7 7.7 %copy-start.9 = (f32[256]{0:T(256)S(1)}, f32[256]{0:T(256)}, u32[]{:S(2)}) copy-start(f32[256]{0:T(256)} %param.21) | copy-start | bytes 3076
  0.7 7.7 %copy-start.5 = (f32[256,128]{1,0:T(8,128)S(1)}, f32[256,128]{1,0:T(8,128)}, u32[]{:S(2)}) copy-start(f32[256,128]{1,0:T(8,128)} %modes_hbm.1) | copy-start | bytes 393220
  0.7 7.7 %copy-start.7 = (f32[256,6]{0,1:T(8,128)S(1)}, f32[256,6]{0,1:T(8,128)}, u32[]{:S(2)}) copy-start(f32[256,6]{0,1:T(8,128)} %param.19) | copy-start | bytes 18436
  0.7 7.7 %copy-start.8 = (s32[1,8,48]{2,1,0:T(8,128)S(1)}, s32[1,8,48]{2,1,0:T(8,128)}, u32[]{:S(2)}) copy-start(s32[1,8,48]{2,1,0:T(8,128)} %param.17) | copy-start | bytes 4612
  2.4 12.3 %collective-permute-start.2 = (f32[3,128]{1,0:T(4,128)}, f32[3,128]{1,0:T(4,128)S(1)}, u32[]{:S(2)}, u32[]{:S(2)}) collective-permute-start(f32[3,128]{1,0:T(4,128)} %get-tuple-element.26), channel_id=1, source_target_pairs={{9,0},{10,1},{11,2},{12,3},{13,4},{14,5},{15,6},{17,8},{18,9},{19,... | collective-permute-start | bytes 4616 | tf_op jit(solution)/shard_map/ppermute | solution.py:490
  3.7 11.0 %collective-permute-start = (f32[3,8,128]{2,1,0:T(8,128)}, f32[3,8,128]{2,1,0:T(8,128)S(1)}, u32[]{:S(2)}, u32[]{:S(2)}) collective-permute-start(f32[3,8,128]{2,1,0:T(8,128)} %get-tuple-element.24), channel_id=1, source_target_pairs={{8,0},{16,8},{24,16},{9,1},{17,9},{25,17},{10,2},{18,10},{26,18},{... | collective-permute-start | bytes 36872 | tf_op jit(solution)/shard_map/ppermute | solution.py:488
  5.0 9.7 %collective-permute-start.1 = (f32[3,24,128]{2,1,0:T(8,128)}, f32[3,24,128]{2,1,0:T(8,128)S(1)}, u32[]{:S(2)}, u32[]{:S(2)}) collective-permute-start(f32[3,24,128]{2,1,0:T(8,128)} %get-tuple-element.25), channel_id=1, source_target_pairs={{1,0},{2,1},{3,2},{4,3},{5,4},{6,5},{7,6},{9,8},{10,9},{11,10},{12... | collective-permute-start | bytes 110600 | tf_op jit(solution)/shard_map/ppermute | solution.py:489
  8.3 6.4 %copy-start = (f32[3,24,8,128]{3,2,1,0:T(8,128)S(1)}, f32[3,24,8,128]{3,2,1,0:T(8,128)}, u32[]{:S(2)}) copy-start(f32[3,24,8,128]{3,2,1,0:T(8,128)} %disp_ref.3) | copy-start | bytes 884740
  8.4 6.4 %copy-start.4 = (f32[1,1,128,48,128]{4,3,2,1,0:T(8,128)S(1)}, f32[1,1,128,48,128]{4,3,2,1,0:T(8,128)}, u32[]{:S(2)}) copy-start(f32[1,1,128,48,128]{4,3,2,1,0:T(8,128)} %param.18) | copy-start | bytes 9437188
  8.4 6.4 %copy-start.6 = (f32[24,8,128]{2,1,0:T(8,128)S(1)}, f32[24,8,128]{2,1,0:T(8,128)}, u32[]{:S(2)}) copy-start(f32[24,8,128]{2,1,0:T(8,128)} %stiff_ref.1) | copy-start | bytes 294916
  18.0 24.4 %collective-permute-start.5 = (f32[3,128]{1,0:T(4,128)S(1)}, f32[3,128]{1,0:T(4,128)S(1)}, u32[]{:S(2)}, u32[]{:S(2)}) collective-permute-start(f32[3,128]{1,0:T(4,128)S(1)} %get-tuple-element.39), channel_id=1, source_target_pairs={{0,9},{1,10},{2,11},{3,12},{4,13},{5,14},{6,15},{8,17},{9,18},{10,... | collective-permute-start | bytes 4616 | tf_op jit(solution)/shard_map/ppermute | solution.py:532
  22.6 19.8 %collective-permute-start.3 = (f32[3,8,128]{2,1,0:T(8,128)S(1)}, f32[3,8,128]{2,1,0:T(8,128)S(1)}, u32[]{:S(2)}, u32[]{:S(2)}) collective-permute-start(f32[3,8,128]{2,1,0:T(8,128)S(1)} %get-tuple-element.37), channel_id=1, source_target_pairs={{0,8},{8,16},{16,24},{1,9},{9,17},{17,25},{2,10},{10,18},{18,26},{... | collective-permute-start | bytes 36872 | tf_op jit(solution)/shard_map/ppermute | solution.py:530
  24.3 18.2 %collective-permute-start.4 = (f32[3,24,128]{2,1,0:T(8,128)S(1)}, f32[3,24,128]{2,1,0:T(8,128)S(1)}, u32[]{:S(2)}, u32[]{:S(2)}) collective-permute-start(f32[3,24,128]{2,1,0:T(8,128)S(1)} %get-tuple-element.38), channel_id=1, source_target_pairs={{0,1},{1,2},{2,3},{3,4},{4,5},{5,6},{6,7},{8,9},{9,10},{10,11},{11... | collective-permute-start | bytes 110600 | tf_op jit(solution)/shard_map/ppermute | solution.py:531
  29.9 12.6 %copy-start.1 = (f32[3,24,8,128]{3,2,1,0:T(8,128)S(1)}, f32[3,24,8,128]{3,2,1,0:T(8,128)}, u32[]{:S(2)}) copy-start(f32[3,24,8,128]{3,2,1,0:T(8,128)} %velocity_ref.1) | copy-start | bytes 884740
  29.9 12.6 %copy-start.2 = (f32[3,24,8,128]{3,2,1,0:T(8,128)S(1)}, f32[3,24,8,128]{3,2,1,0:T(8,128)}, u32[]{:S(2)}) copy-start(f32[3,24,8,128]{3,2,1,0:T(8,128)} %external_ref.1) | copy-start | bytes 884740
  29.9 12.6 %copy-start.3 = (f32[24,8,128]{2,1,0:T(8,128)S(1)}, f32[24,8,128]{2,1,0:T(8,128)}, u32[]{:S(2)}) copy-start(f32[24,8,128]{2,1,0:T(8,128)} %mass_ref.1) | copy-start | bytes 294916
where the time goes:
time: 43 us; the launch traced here: 43.4 us
  Pallas kernels  24.7 us (57%)
  starting transfers between devices  17.7 us (41%)
  between operations  0.94 us (2%)
    pallas_call x1, Pallas kernels, on_device(): pl.pallas_call(functools.partial(inner_kernel, rows, columns), out_shape=...  12.5 us
    pallas_call x1, Pallas kernels, on_device(): pl.pallas_call(functools.partial(matrices_kernel, rows, columns), out_sha...  6.33 us
    ppermute x1, starting transfers between devices, on_device(): yface = lax.ppermute(yface, 'gy', back(along_y))  5.58 us
    ppermute x1, starting transfers between devices, on_device(): cface = lax.ppermute(cface, ('gx', 'gy'), back(both))  4.61 us
    ppermute x1, starting transfers between devices, on_device(): yhalo = lax.ppermute(yhalo, 'gy', along_y)  3.28 us
    pallas_call x1, Pallas kernels, on_device(): pl.pallas_call(functools.partial(edge_kernel, group), out_shape=(shape(3,...  3.24 us
    pallas_call x1, Pallas kernels, on_device(): pl.pallas_call(edges_kernel, out_shape=(shape(3, columns, layers), shape(...  1.69 us
    ppermute x1, starting transfers between devices, on_device(): xface = lax.ppermute(xface, 'gx', back(along_x))  1.62 us
  transfers between devices with their start and end apart: 6, of which 0 were waited for; matrix products, arithmetic and copies ran while one was open for 0% of the time, Pallas kernels for 43%

commit v1 on v0

--- a/solution.py
+++ b/solution.py
@@ -151,9 +151,8 @@
 
 
 def matrices_kernel(
-    rows, columns,
-    modes_hbm, local_hbm, weight_hbm, modulus_hbm, soft_hbm, lists_ref,
-    start0_ref, start1_ref, high_ref, low_ref, back_ref, stress_ref, order_ref,
+    modes_hbm, local_hbm, weight_hbm, modulus_hbm, soft_hbm,
+    start0_ref, start1_ref, high_ref, low_ref, back_ref, stress_ref,
     wide, modes_ref, local_ref, weight_ref, modulus_ref, soft_ref, sems,
 ):
     fetch(
@@ -162,7 +161,6 @@
         sems,
     )
     points, count = modes_ref.shape
-    order_entries(rows, columns, lists_ref, order_ref)
     modes = modes_ref[...]
     modes_t = modes.T
     weight = weight_ref[...] / points
@@ -296,8 +294,11 @@
     return lax.div(order_ref[0, most] + (group - 1), group)
 
 
-def edges_kernel(disp_hbm, xface_ref, yface_ref, corner_ref, disp_ref, sems):
-    fetch((disp_hbm,), (disp_ref,), sems)
+def edges_kernel(disp_hbm, lists_ref, xface_ref, yface_ref, corner_ref, order_ref, disp_ref, sem):
+    copy = pltpu.make_async_copy(disp_hbm, disp_ref, sem)
+    copy.start()
+    order_entries(disp_ref.shape[1], disp_ref.shape[2], lists_ref, order_ref)
+    copy.wait()
     for c in range(3):
         xface_ref[c] = disp_ref[c, 0]
         yface_ref[c] = disp_ref[c, :, 0, :]
@@ -319,9 +320,13 @@
     last_lane = lane == layers - 1
     last_sub = sub == columns - 1
 
+    more_x = lax.axis_index("gx") < lax.axis_size("gx") - 1
+    more_y = lax.axis_index("gy") < lax.axis_size("gy") - 1
+
     def node_row(c, i):
-        own = disp_ref[c, i] if i < rows else xhalo_ref[c]
-        edge = yhalo_ref[c, i : i + 1] if i < rows else corner_ref[c : c + 1]
+        own = disp_ref[c, i] if i < rows else jnp.where(more_x, xhalo_ref[c], 0.0)
+        edge = yhalo_ref[c, i : i + 1] if i < rows else jnp.where(more_x, corner_ref[c : c + 1], 0.0)
+        edge = jnp.where(more_y, edge, 0.0)
         up = jnp.where(last_sub, jnp.broadcast_to(edge, tile), pltpu.roll(own, columns - 1, 0))
         mean, diff = 0.5 * (up + own), up - own
         mean_up = jnp.where(last_lane, 0.0, pltpu.roll(mean, layers - 1, 1))
@@ -442,18 +447,20 @@
     disp_out, velocity_out,
 ):
     rows, columns, layers = mass_ref.shape
+    less_x = lax.axis_index("gx") > 0
     first_sub = lax.broadcasted_iota(jnp.int32, (columns, layers), 0) == 0
+    first_sub = jnp.logical_and(first_sub, lax.axis_index("gy") > 0)
     for i in range(rows):
         factor = STEP / mass_ref[i]
         for c in range(3):
             edge = yface_ref[c, i : i + 1]
             if i == 0:
-                edge = edge + cface_ref[c : c + 1]
+                edge = edge + jnp.where(less_x, cface_ref[c : c + 1], 0.0)
             internal = force_ref[c, i] + jnp.where(
                 first_sub, jnp.broadcast_to(edge, (columns, layers)), 0.0
             )
             if i == 0:
-                internal = internal + xface_ref[c]
+                internal = internal + jnp.where(less_x, xface_ref[c], 0.0)
             velocity = velocity_ref[c, i] + factor * (external_ref[c, i] - internal)
             velocity_out[c, i] = velocity
             disp_out[c, i] = disp_ref[c, i] + STEP * velocity
@@ -471,33 +478,33 @@
     points, count = modes.shape
     most = cloak_list.shape[2]
     gx, gy = lax.axis_size("gx"), lax.axis_size("gy")
-    along_x = [(i + 1, i) for i in range(gx - 1)]
-    along_y = [(i + 1, i) for i in range(gy - 1)]
-    both = [((i + 1) * gy + j + 1, i * gy + j) for i in range(gx - 1) for j in range(gy - 1)]
+    along_x = [((i + 1) % gx, i) for i in range(gx)]
+    along_y = [((j + 1) % gy, j) for j in range(gy)]
+    both = [((i + 1) % gx * gy + (j + 1) % gy, i * gy + j) for i in range(gx) for j in range(gy)]
     back = lambda pairs: [(b, a) for a, b in pairs]
     group = 8
-    xhalo, yhalo, corner = pl.pallas_call(
+    xhalo, yhalo, corner, order = pl.pallas_call(
         edges_kernel,
-        out_shape=(shape(3, columns, layers), shape(3, rows, layers), shape(3, layers)),
-        in_specs=[HBM],
-        out_specs=(VMEM,) * 3,
-        scratch_shapes=[pltpu.VMEM(displacement.shape, F32), pltpu.SemaphoreType.DMA((1,))],
+        out_shape=(
+            shape(3, columns, layers), shape(3, rows, layers), shape(3, layers),
+            shape(2, most + 2, dtype=jnp.int32),
+        ),
+        in_specs=[HBM, SMEM],
+        out_specs=(VMEM,) * 3 + (SMEM,),
+        scratch_shapes=[pltpu.VMEM(displacement.shape, F32), pltpu.SemaphoreType.DMA],
         compiler_params=pltpu.CompilerParams(vmem_limit_bytes=GRANT),
         cost_estimate=pl.CostEstimate(flops=10**10, bytes_accessed=10**6, transcendentals=0),
-    )(displacement)
+    )(displacement, cloak_list[0])
     xhalo = lax.ppermute(xhalo, "gx", along_x)
     yhalo = lax.ppermute(yhalo, "gy", along_y)
     corner = lax.ppermute(corner, ("gx", "gy"), both)
 
-    *matrices, order = pl.pallas_call(
-        functools.partial(matrices_kernel, rows, columns),
+    matrices = pl.pallas_call(
+        matrices_kernel,
         out_shape=tuple(shape(n, points, dtype=BF16) for n in (2 * count, 2 * count, points, points))
-        + (
-            shape(points, 2 * count, dtype=BF16), shape(16, points, dtype=BF16),
-            shape(2, most + 2, dtype=jnp.int32),
-        ),
-        in_specs=[HBM] * 5 + [SMEM],
-        out_specs=(VMEM,) * 6 + (SMEM,),
+        + (shape(points, 2 * count, dtype=BF16), shape(16, points, dtype=BF16)),
+        in_specs=[HBM] * 5,
+        out_specs=(VMEM,) * 6,
         scratch_shapes=[
             pltpu.VMEM((16, points), F32), pltpu.VMEM((points, count), F32),
             pltpu.VMEM((localization.shape[1], points), F32),
@@ -508,7 +515,7 @@
         cost_estimate=pl.CostEstimate(flops=10**10, bytes_accessed=10**6, transcendentals=0),
     )(
         modes, localization.T, point_weight.reshape(1, points), point_modulus.reshape(1, points),
-        softening.reshape(1, points), cloak_list[0],
+        softening.reshape(1, points),
     )
 
     groups = most // group

time: 43 us -> 33.5 us (0.78)
  the two profiles are of different devices: /device:TPU:16 before, /device:TPU:5 now
where the time goes in v1:
time: 33.5 us
  Pallas kernels  24.1 us (72%)
  starting transfers between devices  8.48 us (25%)
  between operations  0.85 us (3%)
    pallas_call x1, Pallas kernels, on_device(): pl.pallas_call(functools.partial(inner_kernel, rows, columns), out_shape=...  10.6 us
    pallas_call x1, Pallas kernels, on_device(): pl.pallas_call(functools.partial(edge_kernel, group), out_shape=(shape(3,...  5.43 us
    ppermute x1, starting transfers between devices, on_device(): corner = lax.ppermute(corner, ('gx', 'gy'), both)  4.86 us
    pallas_call x1, Pallas kernels, on_device(): pl.pallas_call(matrices_kernel, out_shape=tuple((shape(n, points, dtype=B...  4.71 us
    ppermute x1, starting transfers between devices, on_device(): cface = lax.ppermute(cface, ('gx', 'gy'), back(both))  3.01 us
    pallas_call x1, Pallas kernels, on_device(): pl.pallas_call(edges_kernel, out_shape=(shape(3, columns, layers), shape(...  2.48 us
    pallas_call x1, Pallas kernels, on_device(): pl.pallas_call(update_kernel, out_shape=(shape(3, rows, columns, layers),...  0.94 us
  transfers between devices with their start and end apart: 6, of which 0 were waited for; matrix products, arithmetic and copies ran while one was open for 0% of the time, Pallas kernels for 46%

profile of v1, /device:TPU:5, one launch (start us, length us, event | category | flops | bytes accessed | tf_op | source)
XLA Modules:
  0.0 33.5 jit_solution(11696399775100661675)
XLA Ops:
  0.6 0.0 copy-start.5
  0.6 0.0 copy-start.7
  0.7 0.0 copy-start.8
  0.7 0.0 copy-start.9
  0.7 0.0 copy-start.10
  0.7 2.5 %shard_map.139 = (f32[3,8,128]{2,1,0:T(8,128)}, f32[3,24,128]{2,1,0:T(8,128)}, f32[3,128]{1,0:T(4,128)}, s32[2,50]{1,0:T(2,128)}) custom-call(f32[3,24,8,128]{3,2,1,0:T(8,128)} %disp_ref.3, s32[8,48]{1,0:T(8,128)} %bitcast.13), custom_call_target="tpu_custom_call" | custom-call | flops 10000000000 | bytes 1000000 | tf_op jit(solution)/shard_map/pallas_call | solution.py:486
  3.2 4.9 %collective-permute-start.2 = (f32[3,128]{1,0:T(4,128)}, f32[3,128]{1,0:T(4,128)S(1)}, u32[]{:S(2)}, u32[]{:S(2)}) collective-permute-start(f32[3,128]{1,0:T(4,128)} %get-tuple-element.26), channel_id=1, source_target_pairs={{9,0},{10,1},{11,2},{12,3},{13,4},{14,5},{15,6},{8,7},{17,8},{18,9... | collective-permute-start | bytes 4616 | tf_op jit(solution)/shard_map/ppermute | solution.py:500
  8.0 0.0 collective-permute-start
  8.0 0.3 collective-permute-start.1
  8.3 0.0 copy-done.5
  8.3 0.0 copy-done.7
  8.3 0.0 copy-done.8
  8.3 0.0 copy-done.9
  8.3 0.0 copy-done.10
  8.3 0.0 copy-start
  8.3 0.0 copy-start.4
  8.3 0.0 copy-start.6
  8.3 0.0 copy-start.11
  8.4 4.7 %shard_map.140 = (bf16[256,256]{1,0:T(8,128)(2,1)S(1)}, bf16[256,256]{1,0:T(8,128)(2,1)S(1)}, bf16[256,256]{1,0:T(8,128)(2,1)S(1)}, bf16[256,256]{1,0:T(8,128)(2...) custom-call(f32[256,128]{1,0:T(8,128)S(1)} %copy-done.5, f32[6,256]{1,0:T(8,128)S(1)} %bitcast.9, ...), custom_call_target="tpu_custom_call" | custom-call | flops 10000000000 | bytes 1000000 | tf_op jit(solution)/shard_map/pallas_call | solution.py:502
  13.1 0.0 collective-permute-done.2.corner_ref
  13.1 0.0 collective-permute-done.xhalo_ref
  13.1 0.0 collective-permute-done.1.yhalo_ref
  13.1 0.0 copy-done
  13.1 0.0 copy-done.4
  13.1 0.0 copy-done.6
  13.1 0.0 copy-done.11
  13.2 5.4 %shard_map.141 = (f32[3,8,128]{2,1,0:T(8,128)S(1)}, f32[3,24,128]{2,1,0:T(8,128)S(1)}, f32[3,128]{1,0:T(4,128)S(1)}, f32[1536,128]{1,0:T(8,128)S(1)}, f32[1544,128]{1,0:T(8,128)S(1)}, /*index=5*/f32[6144,128]{1,0:T(8,128)S(1)}) custom-call(s32[2,50]{1,0:T(2,128)S(1)} %copy-done.11, f32[3,24,8,128]{3,2,1,0:T(8,128)S(1)} %copy-done, ...), custom_call_target="tpu_custom_call" | custom-call | flops 10000000000 | bytes 10000000 | tf_op jit(solution)/shard_map/pallas_call | solution.py:525
  18.6 3.0 %collective-permute-start.5 = (f32[3,128]{1,0:T(4,128)S(1)}, f32[3,128]{1,0:T(4,128)S(1)}, u32[]{:S(2)}, u32[]{:S(2)}) collective-permute-start(f32[3,128]{1,0:T(4,128)S(1)} %get-tuple-element.39), channel_id=1, source_target_pairs={{0,9},{1,10},{2,11},{3,12},{4,13},{5,14},{6,15},{7,8},{8,17},{9,18... | collective-permute-start | bytes 4616 | tf_op jit(solution)/shard_map/ppermute | solution.py:539
  21.6 0.0 collective-permute-start.3
  21.6 0.3 %collective-permute-start.4 = (f32[3,24,128]{2,1,0:T(8,128)S(1)}, f32[3,24,128]{2,1,0:T(8,128)S(1)}, u32[]{:S(2)}, u32[]{:S(2)}) collective-permute-start(f32[3,24,128]{2,1,0:T(8,128)S(1)} %get-tuple-element.38), channel_id=1, source_target_pairs={{0,1},{1,2},{2,3},{3,4},{4,5},{5,6},{6,7},{7,0},{8,9},{9,10},{10,1... | collective-permute-start | bytes 110600 | tf_op jit(solution)/shard_map/ppermute | solution.py:538
  21.9 0.0 copy-start.1
  21.9 0.0 copy-start.2
  21.9 0.0 copy-start.3
  22.0 10.6 %shard_map.142 = (f32[3,24,8,128]{3,2,1,0:T(8,128)S(1)}, f32[128,48,128]{2,1,0:T(8,128)}) custom-call(s32[2,50]{1,0:T(2,128)S(1)} %copy-done.11, f32[6144,128]{1,0:T(8,128)S(1)} %bitcast.8, f32[1536,128]{1,0:T(8,128)S(1)} %get-tuple-element.33.strain_ref, f32[1544,128]{1,0:T(8,128)S(1)} %get-tuple-element.34.stress_in, ...), custom_call_target="tpu_custom_call" | custom-call | flops 20000000000 | bytes 10000000 | tf_op jit(solution)/shard_map/pallas_call | solution.py:541
  32.5 0.0 collective-permute-done.5.cface_ref
  32.6 0.0 collective-permute-done.3.xface_ref
  32.6 0.0 collective-permute-done.4.yface_ref
  32.6 0.0 copy-done.1
  32.6 0.0 copy-done.2
  32.6 0.0 copy-done.3
  32.6 0.9 %shard_map.143 = (f32[3,24,8,128]{3,2,1,0:T(8,128)}, f32[3,24,8,128]{3,2,1,0:T(8,128)}) custom-call(f32[3,24,8,128]{3,2,1,0:T(8,128)S(1)} %copy-done, f32[3,24,8,128]{3,2,1,0:T(8,128)S(1)} %copy-done.1, f32[3,24,8,128]{3,2,1,0:T(8,128)S(1)} %copy-done.2, f32[24,8,128]{2,1,0:T(8,128)S(1)} %copy-done.3, f32[3,24,8,128]{3,2,1,0:T(8,128)S(1)} %get-tuple-element.36.force_ref, ...), custom_call_target="tpu_custom_call" | custom-call | tf_op jit(solution)/shard_map/pallas_call | solution.py:554
Async XLA Ops:
  0.6 7.7 %copy-start.5 = (f32[256,128]{1,0:T(8,128)S(1)}, f32[256,128]{1,0:T(8,128)}, u32[]{:S(2)}) copy-start(f32[256,128]{1,0:T(8,128)} %modes_hbm.1) | copy-start | bytes 393220
  0.6 7.7 %copy-start.7 = (f32[256,6]{0,1:T(8,128)S(1)}, f32[256,6]{0,1:T(8,128)}, u32[]{:S(2)}) copy-start(f32[256,6]{0,1:T(8,128)} %param.19) | copy-start | bytes 18436
  0.7 7.6 %copy-start.8 = (f32[256]{0:T(256)S(1)}, f32[256]{0:T(256)}, u32[]{:S(2)}) copy-start(f32[256]{0:T(256)} %param.21) | copy-start | bytes 3076
  0.7 7.6 %copy-start.9 = (f32[256]{0:T(256)S(1)}, f32[256]{0:T(256)}, u32[]{:S(2)}) copy-start(f32[256]{0:T(256)} %param.22) | copy-start | bytes 3076
  0.7 7.6 %copy-start.10 = (f32[256]{0:T(256)S(1)}, f32[256]{0:T(256)}, u32[]{:S(2)}) copy-start(f32[256]{0:T(256)} %param.23) | copy-start | bytes 3076
  3.2 9.9 %collective-permute-start.2 = (f32[3,128]{1,0:T(4,128)}, f32[3,128]{1,0:T(4,128)S(1)}, u32[]{:S(2)}, u32[]{:S(2)}) collective-permute-start(f32[3,128]{1,0:T(4,128)} %get-tuple-element.26), channel_id=1, source_target_pairs={{9,0},{10,1},{11,2},{12,3},{13,4},{14,5},{15,6},{8,7},{17,8},{18,9... | collective-permute-start | bytes 4616 | tf_op jit(solution)/shard_map/ppermute | solution.py:500
  8.0 5.1 %collective-permute-start = (f32[3,8,128]{2,1,0:T(8,128)}, f32[3,8,128]{2,1,0:T(8,128)S(1)}, u32[]{:S(2)}, u32[]{:S(2)}) collective-permute-start(f32[3,8,128]{2,1,0:T(8,128)} %get-tuple-element.24), channel_id=1, source_target_pairs={{8,0},{16,8},{24,16},{0,24},{9,1},{17,9},{25,17},{1,25},{10,2},{18... | collective-permute-start | bytes 36872 | tf_op jit(solution)/shard_map/ppermute | solution.py:498
  8.0 5.1 %collective-permute-start.1 = (f32[3,24,128]{2,1,0:T(8,128)}, f32[3,24,128]{2,1,0:T(8,128)S(1)}, u32[]{:S(2)}, u32[]{:S(2)}) collective-permute-start(f32[3,24,128]{2,1,0:T(8,128)} %get-tuple-element.25), channel_id=1, source_target_pairs={{1,0},{2,1},{3,2},{4,3},{5,4},{6,5},{7,6},{0,7},{9,8},{10,9},{11,1... | collective-permute-start | bytes 110600 | tf_op jit(solution)/shard_map/ppermute | solution.py:499
  8.3 4.8 %copy-start = (f32[3,24,8,128]{3,2,1,0:T(8,128)S(1)}, f32[3,24,8,128]{3,2,1,0:T(8,128)}, u32[]{:S(2)}) copy-start(f32[3,24,8,128]{3,2,1,0:T(8,128)} %disp_ref.3) | copy-start | bytes 884740
  8.3 4.8 %copy-start.4 = (f32[1,1,128,48,128]{4,3,2,1,0:T(8,128)S(1)}, f32[1,1,128,48,128]{4,3,2,1,0:T(8,128)}, u32[]{:S(2)}) copy-start(f32[1,1,128,48,128]{4,3,2,1,0:T(8,128)} %param.18) | copy-start | bytes 9437188
  8.3 4.8 %copy-start.6 = (f32[24,8,128]{2,1,0:T(8,128)S(1)}, f32[24,8,128]{2,1,0:T(8,128)}, u32[]{:S(2)}) copy-start(f32[24,8,128]{2,1,0:T(8,128)} %stiff_ref.1) | copy-start | bytes 294916
  8.3 4.8 %copy-start.11 = (s32[2,50]{1,0:T(2,128)S(1)}, s32[2,50]{1,0:T(2,128)}, u32[]{:S(2)}) copy-start(s32[2,50]{1,0:T(2,128)} %get-tuple-element.23.order_ref) | copy-start | bytes 1204
  18.6 14.0 %collective-permute-start.5 = (f32[3,128]{1,0:T(4,128)S(1)}, f32[3,128]{1,0:T(4,128)S(1)}, u32[]{:S(2)}, u32[]{:S(2)}) collective-permute-start(f32[3,128]{1,0:T(4,128)S(1)} %get-tuple-element.39), channel_id=1, source_target_pairs={{0,9},{1,10},{2,11},{3,12},{4,13},{5,14},{6,15},{7,8},{8,17},{9,18... | collective-permute-start | bytes 4616 | tf_op jit(solution)/shard_map/ppermute | solution.py:539
  21.6 11.0 %collective-permute-start.3 = (f32[3,8,128]{2,1,0:T(8,128)S(1)}, f32[3,8,128]{2,1,0:T(8,128)S(1)}, u32[]{:S(2)}, u32[]{:S(2)}) collective-permute-start(f32[3,8,128]{2,1,0:T(8,128)S(1)} %get-tuple-element.37), channel_id=1, source_target_pairs={{0,8},{8,16},{16,24},{24,0},{1,9},{9,17},{17,25},{25,1},{2,10},{10... | collective-permute-start | bytes 36872 | tf_op jit(solution)/shard_map/ppermute | solution.py:537
  21.6 11.0 %collective-permute-start.4 = (f32[3,24,128]{2,1,0:T(8,128)S(1)}, f32[3,24,128]{2,1,0:T(8,128)S(1)}, u32[]{:S(2)}, u32[]{:S(2)}) collective-permute-start(f32[3,24,128]{2,1,0:T(8,128)S(1)} %get-tuple-element.38), channel_id=1, source_target_pairs={{0,1},{1,2},{2,3},{3,4},{4,5},{5,6},{6,7},{7,0},{8,9},{9,10},{10,1... | collective-permute-start | bytes 110600 | tf_op jit(solution)/shard_map/ppermute | solution.py:538
  21.9 10.6 %copy-start.1 = (f32[3,24,8,128]{3,2,1,0:T(8,128)S(1)}, f32[3,24,8,128]{3,2,1,0:T(8,128)}, u32[]{:S(2)}) copy-start(f32[3,24,8,128]{3,2,1,0:T(8,128)} %velocity_ref.1) | copy-start | bytes 884740
  21.9 10.6 %copy-start.2 = (f32[3,24,8,128]{3,2,1,0:T(8,128)S(1)}, f32[3,24,8,128]{3,2,1,0:T(8,128)}, u32[]{:S(2)}) copy-start(f32[3,24,8,128]{3,2,1,0:T(8,128)} %external_ref.1) | copy-start | bytes 884740
  21.9 10.6 %copy-start.3 = (f32[24,8,128]{2,1,0:T(8,128)S(1)}, f32[24,8,128]{2,1,0:T(8,128)}, u32[]{:S(2)}) copy-start(f32[24,8,128]{2,1,0:T(8,128)} %mass_ref.1) | copy-start | bytes 294916

commit v2 on v1

--- a/solution.py
+++ b/solution.py
@@ -12,10 +12,8 @@
 HIGHEST = lax.Precision.HIGHEST
 F32 = jnp.float32
 BF16 = jnp.bfloat16
-GRANT = 60 * 2**20
 VMEM = pl.BlockSpec(memory_space=pltpu.VMEM)
 HBM = pl.BlockSpec(memory_space=pltpu.HBM)
-SMEM = pl.BlockSpec(memory_space=pltpu.SMEM)
 
 
 def split(x):
@@ -117,49 +115,46 @@
     return dot(ah, bh) + dot(al, bh) + dot(ah, bl)
 
 
-def fetch(sources, targets, sems):
-    copies = [
-        pltpu.make_async_copy(a, b, sems.at[i]) for i, (a, b) in enumerate(zip(sources, targets))
-    ]
-    for copy in copies:
-        copy.start()
-    for copy in copies:
-        copy.wait()
-
-
-def order_entries(rows, columns, lists_ref, order_ref):
-    member = lax.axis_index("gy")
+def order_entries(rows, columns, lists_ref, order_ref, line):
     most = lists_ref.shape[1]
-    pencils = [lists_ref[member, e] for e in range(most)]
-    listed = [(p >= 0).astype(jnp.int32) for p in pencils]
-    edge = [
-        jnp.logical_or(p >= (rows - 1) * columns, lax.rem(p, columns) == columns - 1).astype(jnp.int32)
-        for p in pencils
-    ]
-    edges, number = sum(edge), sum(listed)
-    next_edge, next_inner, next_rest = 0, edges, number
-    for e in range(most):
-        inner = listed[e] - edge[e]
-        place = jnp.where(edge[e] > 0, next_edge, jnp.where(inner > 0, next_inner, next_rest))
-        order_ref[0, place] = e
-        order_ref[1, place] = pencils[e]
-        next_edge = next_edge + edge[e]
-        next_inner = next_inner + inner
-        next_rest = next_rest + (1 - listed[e])
-    order_ref[0, most] = edges
-    order_ref[0, most + 1] = number
+    width = order_ref.shape[1]
+    tile = order_ref.shape
+    line[...] = jnp.full(line.shape, -1, jnp.int32)
+    line[0:1, 0:most] = lists_ref[pl.ds(lax.axis_index("gy"), 1), :]
+    pencil = jnp.broadcast_to(line[0:1, :].astype(F32), tile)
+    lane = lax.broadcasted_iota(jnp.int32, tile, 1)
+    row = lax.broadcasted_iota(jnp.int32, tile, 0)
+    column = pencil - columns * jnp.floor((pencil + 0.5) / columns)
+    listed = pencil >= 0.0
+    face = jnp.logical_or(pencil >= (rows - 1) * columns, column == columns - 1)
+    kind = jnp.where(listed, jnp.where(face, 0, 1), jnp.where(lane < most, 2, 3))
+    flags = jnp.where(kind == row, 1.0, 0.0).astype(BF16)
+    square = (width, width)
+    first = lax.broadcasted_iota(jnp.int32, square, 0)
+    second = lax.broadcasted_iota(jnp.int32, square, 1)
+    before = dot(flags, (first < second).astype(F32).astype(BF16))
+    totals = dot(flags, jnp.ones(square, BF16))
+    faces, number = totals[0:1], totals[0:1] + totals[1:2]
+    kind = kind[0:1]
+    place = jnp.where(
+        kind == 0, before[0:1],
+        jnp.where(kind == 1, faces + before[1:2], jnp.where(kind == 2, number + before[2:3], -1.0)),
+    )
+    moves = (jnp.broadcast_to(place, square) == first.astype(F32)).astype(F32)
+    values = jnp.where(row == 0, lane.astype(F32), pencil)
+    ordered = lax.dot_general(
+        values, moves, (((1,), (1,)), ((), ())), precision=HIGHEST, preferred_element_type=F32
+    )
+    counts = jnp.where(lane == most, jnp.broadcast_to(faces, tile), jnp.broadcast_to(number, tile))
+    tail = jnp.logical_and(row == 0, lane >= most)
+    order_ref[...] = jnp.where(tail, counts, ordered).astype(jnp.int32)
 
 
 def matrices_kernel(
-    modes_hbm, local_hbm, weight_hbm, modulus_hbm, soft_hbm,
-    start0_ref, start1_ref, high_ref, low_ref, back_ref, stress_ref,
-    wide, modes_ref, local_ref, weight_ref, modulus_ref, soft_ref, sems,
+    rows, columns, modes_ref, local_ref, weight_ref, modulus_ref, soft_ref, lists_ref,
+    start0_ref, start1_ref, high_ref, low_ref, back_ref, stress_ref, order_ref, wide, line,
 ):
-    fetch(
-        (modes_hbm, local_hbm, weight_hbm, modulus_hbm, soft_hbm),
-        (modes_ref, local_ref, weight_ref, modulus_ref, soft_ref),
-        sems,
-    )
+    order_entries(rows, columns, lists_ref, order_ref, line)
     points, count = modes_ref.shape
     modes = modes_ref[...]
     modes_t = modes.T
@@ -294,11 +289,7 @@
     return lax.div(order_ref[0, most] + (group - 1), group)
 
 
-def edges_kernel(disp_hbm, lists_ref, xface_ref, yface_ref, corner_ref, order_ref, disp_ref, sem):
-    copy = pltpu.make_async_copy(disp_hbm, disp_ref, sem)
-    copy.start()
-    order_entries(disp_ref.shape[1], disp_ref.shape[2], lists_ref, order_ref)
-    copy.wait()
+def edges_kernel(disp_ref, xface_ref, yface_ref, corner_ref):
     for c in range(3):
         xface_ref[c] = disp_ref[c, 0]
         yface_ref[c] = disp_ref[c, :, 0, :]
@@ -306,12 +297,14 @@
 
 
 def edge_kernel(
-    group, order_ref, disp_ref, xhalo_ref, yhalo_ref, corner_ref, stiff_ref, state_ref,
+    group, most, order_vmem, disp_ref, xhalo_ref, yhalo_ref, corner_ref, stiff_ref, state_ref,
     start0_ref, start1_ref, high_ref, low_ref, back_ref, stress_ref,
     xface_ref, yface_ref, cface_ref, strain_ref, stress_out, done_ref,
+    order_ref, order_sem,
 ):
+    order_copy = pltpu.make_async_copy(order_vmem, order_ref, order_sem)
+    order_copy.start()
     rows, columns, layers = stiff_ref.shape
-    most = order_ref.shape[1] - 2
     count = state_ref.shape[0] // most
     weights = (start0_ref, start1_ref, high_ref, low_ref, back_ref, stress_ref)
     tile = (columns, layers)
@@ -353,6 +346,8 @@
             strain_ref[place, :] = strain[c]
             stress_out[place, :] = stiffness * (volume + 2.0 * strain[c] if c < 3 else strain[c])
 
+    order_copy.wait()
+
     def body(q, carry):
         _, states = run_group(
             q * group, group, order_ref, state_ref, strain_ref, weights, stress_out, rows * columns
@@ -375,17 +370,20 @@
 
 
 def inner_kernel(
-    rows, columns, order_ref, state_ref, strain_ref, stress_in, done_ref,
+    rows, columns, order_vmem, state_ref, strain_ref, stress_in, done_ref,
     start0_ref, start1_ref, high_ref, low_ref, back_ref, stress_ref,
     force_ref, out_hbm,
-    stress_s, out_s, sems,
+    stress_s, out_s, sems, order_ref, order_sem,
 ):
+    order_copy = pltpu.make_async_copy(order_vmem, order_ref, order_sem)
+    order_copy.start()
     groups, count, group, layers = out_s.shape
     most = groups * group
     weights = (start0_ref, start1_ref, high_ref, low_ref, back_ref, stress_ref)
+    stress_s[...] = stress_in[...]
+    order_copy.wait()
     before = first_groups(order_ref, most, group)
     after = lax.div(order_ref[0, most + 1] + (group - 1), group)
-    stress_s[...] = stress_in[...]
 
     def store(q):
         return pltpu.make_async_copy(
@@ -483,39 +481,31 @@
     both = [((i + 1) % gx * gy + (j + 1) % gy, i * gy + j) for i in range(gx) for j in range(gy)]
     back = lambda pairs: [(b, a) for a, b in pairs]
     group = 8
-    xhalo, yhalo, corner, order = pl.pallas_call(
+    xhalo, yhalo, corner = pl.pallas_call(
         edges_kernel,
-        out_shape=(
-            shape(3, columns, layers), shape(3, rows, layers), shape(3, layers),
-            shape(2, most + 2, dtype=jnp.int32),
-        ),
-        in_specs=[HBM, SMEM],
-        out_specs=(VMEM,) * 3 + (SMEM,),
-        scratch_shapes=[pltpu.VMEM(displacement.shape, F32), pltpu.SemaphoreType.DMA],
-        compiler_params=pltpu.CompilerParams(vmem_limit_bytes=GRANT),
+        out_shape=(shape(3, columns, layers), shape(3, rows, layers), shape(3, layers)),
+        in_specs=[VMEM],
+        out_specs=(VMEM,) * 3,
+        compiler_params=pltpu.CompilerParams(vmem_limit_bytes=4 * 2**20),
         cost_estimate=pl.CostEstimate(flops=10**10, bytes_accessed=10**6, transcendentals=0),
-    )(displacement, cloak_list[0])
+    )(displacement)
     xhalo = lax.ppermute(xhalo, "gx", along_x)
     yhalo = lax.ppermute(yhalo, "gy", along_y)
     corner = lax.ppermute(corner, ("gx", "gy"), both)
 
-    matrices = pl.pallas_call(
-        matrices_kernel,
+    order_shape = shape(8, (most + 2 + 127) // 128 * 128, dtype=jnp.int32)
+    *matrices, order = pl.pallas_call(
+        functools.partial(matrices_kernel, rows, columns),
         out_shape=tuple(shape(n, points, dtype=BF16) for n in (2 * count, 2 * count, points, points))
-        + (shape(points, 2 * count, dtype=BF16), shape(16, points, dtype=BF16)),
-        in_specs=[HBM] * 5,
-        out_specs=(VMEM,) * 6,
-        scratch_shapes=[
-            pltpu.VMEM((16, points), F32), pltpu.VMEM((points, count), F32),
-            pltpu.VMEM((localization.shape[1], points), F32),
-        ]
-        + [pltpu.VMEM((1, points), F32)] * 3
-        + [pltpu.SemaphoreType.DMA((5,))],
+        + (shape(points, 2 * count, dtype=BF16), shape(16, points, dtype=BF16), order_shape),
+        in_specs=[VMEM] * 6,
+        out_specs=(VMEM,) * 7,
+        scratch_shapes=[pltpu.VMEM((16, points), F32), pltpu.VMEM(order_shape.shape, jnp.int32)],
         compiler_params=pltpu.CompilerParams(vmem_limit_bytes=16 * 2**20),
         cost_estimate=pl.CostEstimate(flops=10**10, bytes_accessed=10**6, transcendentals=0),
     )(
         modes, localization.T, point_weight.reshape(1, points), point_modulus.reshape(1, points),
-        softening.reshape(1, points),
+        softening.reshape(1, points), cloak_list[0],
     )
 
     groups = most // group
@@ -523,13 +513,14 @@
     strain_shape = shape(rows * columns * 8, layers)
     stress_shape = shape(rows * columns * 8 + 8, layers)
     xface, yface, cface, strain, stress, done = pl.pallas_call(
-        functools.partial(edge_kernel, group),
+        functools.partial(edge_kernel, group, most),
         out_shape=(
             shape(3, columns, layers), shape(3, rows, layers), shape(3, layers),
             strain_shape, stress_shape, shape(most * count, layers),
         ),
-        in_specs=[SMEM] + [VMEM] * 12,
+        in_specs=[VMEM] * 13,
         out_specs=(VMEM,) * 6,
+        scratch_shapes=[pltpu.SMEM(order_shape.shape, jnp.int32), pltpu.SemaphoreType.DMA],
         compiler_params=pltpu.CompilerParams(vmem_limit_bytes=30 * 2**20),
         cost_estimate=pl.CostEstimate(flops=10**10, bytes_accessed=10**7, transcendentals=0),
     )(order, displacement, xhalo, yhalo, corner, stiffness, states, *matrices)
@@ -541,11 +532,12 @@
     force, new_state = pl.pallas_call(
         functools.partial(inner_kernel, rows, columns),
         out_shape=(shape(3, rows, columns, layers), shape(count, most, layers)),
-        in_specs=[SMEM] + [VMEM] * 10,
+        in_specs=[VMEM] * 11,
         out_specs=(VMEM, HBM),
         scratch_shapes=[
             pltpu.VMEM(stress_shape.shape, F32), pltpu.VMEM((groups, count, group, layers), F32),
             pltpu.SemaphoreType.DMA((groups,)),
+            pltpu.SMEM(order_shape.shape, jnp.int32), pltpu.SemaphoreType.DMA,
         ],
         compiler_params=pltpu.CompilerParams(vmem_limit_bytes=30 * 2**20),
         cost_estimate=pl.CostEstimate(flops=2 * 10**10, bytes_accessed=10**7, transcendentals=0),

time: 33.5 us -> 31.9 us (0.952)
  the two profiles are of different devices: /device:TPU:5 before, /device:TPU:1 now
where the time goes in v2:
time: 31.9 us; the launch traced here: 32.3 us
  Pallas kernels  21.2 us (66%)
  starting transfers between devices  9.28 us (29%)
  local copies, waits for them, and re-layouts  1.01 us (3%)
  between operations  0.84 us (3%)
    pallas_call x1, Pallas kernels, on_device(): pl.pallas_call(functools.partial(inner_kernel, rows, columns), out_shape=...  12.5 us
    ppermute x1, starting transfers between devices, on_device(): corner = lax.ppermute(corner, ('gx', 'gy'), both)  5.69 us
    pallas_call x1, Pallas kernels, on_device(): pl.pallas_call(functools.partial(matrices_kernel, rows, columns), out_sha...  4.54 us
    pallas_call x1, Pallas kernels, on_device(): pl.pallas_call(functools.partial(edge_kernel, group, most), out_shape=(sh...  3.17 us
    ppermute x1, starting transfers between devices, on_device(): cface = lax.ppermute(cface, ('gx', 'gy'), back(both))  2.2 us
    unnamed x26, local copies, waits for them, and re-layouts  1.01 us
    pallas_call x1, Pallas kernels, on_device(): pl.pallas_call(update_kernel, out_shape=(shape(3, rows, columns, layers),...  0.94 us
    ppermute x1, starting transfers between devices, on_device(): xhalo = lax.ppermute(xhalo, 'gx', along_x)  0.79 us
  transfers between devices with their start and end apart: 6, of which 0 were waited for; matrix products, arithmetic and copies ran while one was open for 0% of the time, Pallas kernels for 53%

profile of v2, /device:TPU:1, one launch (start us, length us, event | category | flops | bytes accessed | tf_op | source)
XLA Modules:
  0.0 32.3 jit_solution(8910059404273644272)
XLA Ops:
  0.6 0.0 copy-start
  0.6 1.0 %copy-done = f32[3,24,8,128]{3,2,1,0:T(8,128)S(1)} copy-done((f32[3,24,8,128]{3,2,1,0:T(8,128)S(1)}, f32[3,24,8,128]{3,2,1,0:T(8,128)}, u32[]{:S(2)}) %copy-start) | copy-done | bytes 294936
  1.6 0.0 copy-start.6
  1.6 0.0 copy-start.8
  1.6 0.0 copy-start.9
  1.6 0.0 copy-start.10
  1.6 0.0 copy-start.11
  1.6 0.0 copy-start.12
  1.7 5.7 %collective-permute-start.2 = (f32[3,128]{1,0:T(4,128)S(1)}, f32[3,128]{1,0:T(4,128)S(1)}, u32[]{:S(2)}, u32[]{:S(2)}) collective-permute-start(f32[3,128]{1,0:T(4,128)S(1)} %get-tuple-element.26), channel_id=1, source_target_pairs={{9,0},{10,1},{11,2},{12,3},{13,4},{14,5},{15,6},{8,7},{17,8},{18,9... | collective-permute-start | bytes 4616 | tf_op jit(solution)/shard_map/ppermute | solution.py:494
  7.4 0.8 %collective-permute-start = (f32[3,8,128]{2,1,0:T(8,128)S(1)}, f32[3,8,128]{2,1,0:T(8,128)S(1)}, u32[]{:S(2)}, u32[]{:S(2)}) collective-permute-start(f32[3,8,128]{2,1,0:T(8,128)S(1)} %get-tuple-element.24), channel_id=1, source_target_pairs={{8,0},{16,8},{24,16},{0,24},{9,1},{17,9},{25,17},{1,25},{10,2},{18... | collective-permute-start | bytes 36872 | tf_op jit(solution)/shard_map/ppermute | solution.py:492
  8.1 0.3 collective-permute-start.1
  8.4 0.0 copy-done.6
  8.4 0.0 copy-done.8
  8.4 0.0 copy-done.9
  8.4 0.0 copy-done.10
  8.4 0.0 copy-done.11
  8.4 0.0 copy-done.12
  8.4 0.0 copy-start.1
  8.4 0.0 copy-start.5
  8.5 0.0 copy-start.7
  8.5 4.5 %shard_map.139 = (bf16[256,256]{1,0:T(8,128)(2,1)S(1)}, bf16[256,256]{1,0:T(8,128)(2,1)S(1)}, bf16[256,256]{1,0:T(8,128)(2,1)S(1)}, bf16[256,256]{1,0:T(8,128)(2...) custom-call(f32[256,128]{1,0:T(8,128)S(1)} %copy-done.6, ...), custom_call_target="tpu_custom_call" | custom-call | flops 10000000000 | bytes 1000000 | tf_op jit(solution)/shard_map/pallas_call | solution.py:497
  13.0 0.0 collective-permute-done.2.corner_ref
  13.0 0.0 collective-permute-done.xhalo_ref
  13.0 0.0 collective-permute-done.1.yhalo_ref
  13.0 0.0 copy-done.1
  13.1 0.0 copy-done.5
  13.1 0.0 copy-done.7
  13.1 3.2 %shard_map.141 = (f32[3,8,128]{2,1,0:T(8,128)S(1)}, f32[3,24,128]{2,1,0:T(8,128)S(1)}, f32[3,128]{1,0:T(4,128)S(1)}, f32[1536,128]{1,0:T(8,128)S(1)}, f32[1544,128]{1,0:T(8,128)S(1)}, /*index=5*/f32[6144,128]{1,0:T(8,128)S(1)}) custom-call(s32[8,128]{1,0:T(8,128)S(1)} %get-tuple-element.23.order_vmem, f32[3,24,8,128]{3,2,1,0:T(8,128)S(1)} %copy-done.1, ...), custom_call_target="tpu_custom_call" | custom-call | flops 10000000000 | bytes 10000000 | tf_op jit(solution)/shard_map/pallas_call | solution.py:515
  16.3 2.2 %collective-permute-start.5 = (f32[3,128]{1,0:T(4,128)S(1)}, f32[3,128]{1,0:T(4,128)S(1)}, u32[]{:S(2)}, u32[]{:S(2)}) collective-permute-start(f32[3,128]{1,0:T(4,128)S(1)} %get-tuple-element.39), channel_id=1, source_target_pairs={{0,9},{1,10},{2,11},{3,12},{4,13},{5,14},{6,15},{7,8},{8,17},{9,18... | collective-permute-start | bytes 4616 | tf_op jit(solution)/shard_map/ppermute | solution.py:530
  18.4 0.0 collective-permute-start.3
  18.5 0.3 %collective-permute-start.4 = (f32[3,24,128]{2,1,0:T(8,128)S(1)}, f32[3,24,128]{2,1,0:T(8,128)S(1)}, u32[]{:S(2)}, u32[]{:S(2)}) collective-permute-start(f32[3,24,128]{2,1,0:T(8,128)S(1)} %get-tuple-element.38), channel_id=1, source_target_pairs={{0,1},{1,2},{2,3},{3,4},{4,5},{5,6},{6,7},{7,0},{8,9},{9,10},{10,1... | collective-permute-start | bytes 110600 | tf_op jit(solution)/shard_map/ppermute | solution.py:529
  18.8 0.0 copy-start.2
  18.8 0.0 copy-start.3
  18.8 0.0 copy-start.4
  18.8 12.5 %shard_map.142 = (f32[3,24,8,128]{3,2,1,0:T(8,128)S(1)}, f32[128,48,128]{2,1,0:T(8,128)}) custom-call(s32[8,128]{1,0:T(8,128)S(1)} %get-tuple-element.23.order_vmem, f32[6144,128]{1,0:T(8,128)S(1)} %bitcast.8, f32[1536,128]{1,0:T(8,128)S(1)} %get-tuple-element.33.strain_ref, f32[1544,128]{1,0:T(8,128)S(1)} %get-tuple-element.34.stress_in, ...), custom_call_target="tpu_custom_call" | custom-call | flops 20000000000 | bytes 10000000 | tf_op jit(solution)/shard_map/pallas_call | solution.py:532
  31.3 0.0 collective-permute-done.5.cface_ref
  31.3 0.0 collective-permute-done.3.xface_ref
  31.4 0.0 collective-permute-done.4.yface_ref
  31.4 0.0 copy-done.2
  31.4 0.0 copy-done.3
  31.4 0.0 copy-done.4
  31.4 0.9 %shard_map.143 = (f32[3,24,8,128]{3,2,1,0:T(8,128)}, f32[3,24,8,128]{3,2,1,0:T(8,128)}) custom-call(f32[3,24,8,128]{3,2,1,0:T(8,128)S(1)} %copy-done.1, f32[3,24,8,128]{3,2,1,0:T(8,128)S(1)} %copy-done.2, f32[3,24,8,128]{3,2,1,0:T(8,128)S(1)} %copy-done.3, f32[24,8,128]{2,1,0:T(8,128)S(1)} %copy-done.4, f32[3,24,8,128]{3,2,1,0:T(8,128)S(1)} %get-tuple-element.36.force_ref, ...), custom_call_target="tpu_custom_call" | custom-call | tf_op jit(solution)/shard_map/pallas_call | solution.py:546
  (1 shorter events, 0.0 us)
Async XLA Ops:
  0.6 1.0 %copy-start = (f32[3,24,8,128]{3,2,1,0:T(8,128)S(1)}, f32[3,24,8,128]{3,2,1,0:T(8,128)}, u32[]{:S(2)}) copy-start(f32[3,24,8,128]{3,2,1,0:T(8,128)} %disp_ref.5) | copy-start | bytes 884740
  1.6 6.8 %copy-start.6 = (f32[256,128]{1,0:T(8,128)S(1)}, f32[256,128]{1,0:T(8,128)}, u32[]{:S(2)}) copy-start(f32[256,128]{1,0:T(8,128)} %modes_ref.1) | copy-start | bytes 393220
  1.6 6.8 %copy-start.8 = (f32[256,6]{0,1:T(8,128)S(1)}, f32[256,6]{0,1:T(8,128)}, u32[]{:S(2)}) copy-start(f32[256,6]{0,1:T(8,128)} %param.19) | copy-start | bytes 18436
  1.6 6.8 %copy-start.9 = (s32[1,8,48]{2,1,0:T(8,128)S(1)}, s32[1,8,48]{2,1,0:T(8,128)}, u32[]{:S(2)}) copy-start(s32[1,8,48]{2,1,0:T(8,128)} %param.17) | copy-start | bytes 4612
  1.6 6.8 %copy-start.10 = (f32[256]{0:T(256)S(1)}, f32[256]{0:T(256)}, u32[]{:S(2)}) copy-start(f32[256]{0:T(256)} %param.21) | copy-start | bytes 3076
  1.6 6.8 %copy-start.11 = (f32[256]{0:T(256)S(1)}, f32[256]{0:T(256)}, u32[]{:S(2)}) copy-start(f32[256]{0:T(256)} %param.22) | copy-start | bytes 3076
  1.6 6.8 %copy-start.12 = (f32[256]{0:T(256)S(1)}, f32[256]{0:T(256)}, u32[]{:S(2)}) copy-start(f32[256]{0:T(256)} %param.23) | copy-start | bytes 3076
  1.7 11.4 %collective-permute-start.2 = (f32[3,128]{1,0:T(4,128)S(1)}, f32[3,128]{1,0:T(4,128)S(1)}, u32[]{:S(2)}, u32[]{:S(2)}) collective-permute-start(f32[3,128]{1,0:T(4,128)S(1)} %get-tuple-element.26), channel_id=1, source_target_pairs={{9,0},{10,1},{11,2},{12,3},{13,4},{14,5},{15,6},{8,7},{17,8},{18,9... | collective-permute-start | bytes 4616 | tf_op jit(solution)/shard_map/ppermute | solution.py:494
  7.4 5.7 %collective-permute-start = (f32[3,8,128]{2,1,0:T(8,128)S(1)}, f32[3,8,128]{2,1,0:T(8,128)S(1)}, u32[]{:S(2)}, u32[]{:S(2)}) collective-permute-start(f32[3,8,128]{2,1,0:T(8,128)S(1)} %get-tuple-element.24), channel_id=1, source_target_pairs={{8,0},{16,8},{24,16},{0,24},{9,1},{17,9},{25,17},{1,25},{10,2},{18... | collective-permute-start | bytes 36872 | tf_op jit(solution)/shard_map/ppermute | solution.py:492
  8.1 4.9 %collective-permute-start.1 = (f32[3,24,128]{2,1,0:T(8,128)S(1)}, f32[3,24,128]{2,1,0:T(8,128)S(1)}, u32[]{:S(2)}, u32[]{:S(2)}) collective-permute-start(f32[3,24,128]{2,1,0:T(8,128)S(1)} %get-tuple-element.25), channel_id=1, source_target_pairs={{1,0},{2,1},{3,2},{4,3},{5,4},{6,5},{7,6},{0,7},{9,8},{10,9},{11,1... | collective-permute-start | bytes 110600 | tf_op jit(solution)/shard_map/ppermute | solution.py:493
  8.4 4.6 %copy-start.1 = (f32[3,24,8,128]{3,2,1,0:T(8,128)S(1)}, f32[3,24,8,128]{3,2,1,0:T(8,128)}, u32[]{:S(2)}) copy-start(f32[3,24,8,128]{3,2,1,0:T(8,128)} %disp_ref.5) | copy-start | bytes 884740
  8.4 4.6 %copy-start.5 = (f32[1,1,128,48,128]{4,3,2,1,0:T(8,128)S(1)}, f32[1,1,128,48,128]{4,3,2,1,0:T(8,128)}, u32[]{:S(2)}) copy-start(f32[1,1,128,48,128]{4,3,2,1,0:T(8,128)} %param.18) | copy-start | bytes 9437188
  8.5 4.6 %copy-start.7 = (f32[24,8,128]{2,1,0:T(8,128)S(1)}, f32[24,8,128]{2,1,0:T(8,128)}, u32[]{:S(2)}) copy-start(f32[24,8,128]{2,1,0:T(8,128)} %stiff_ref.1) | copy-start | bytes 294916
  16.3 15.1 %collective-permute-start.5 = (f32[3,128]{1,0:T(4,128)S(1)}, f32[3,128]{1,0:T(4,128)S(1)}, u32[]{:S(2)}, u32[]{:S(2)}) collective-permute-start(f32[3,128]{1,0:T(4,128)S(1)} %get-tuple-element.39), channel_id=1, source_target_pairs={{0,9},{1,10},{2,11},{3,12},{4,13},{5,14},{6,15},{7,8},{8,17},{9,18... | collective-permute-start | bytes 4616 | tf_op jit(solution)/shard_map/ppermute | solution.py:530
  18.4 12.9 %collective-permute-start.3 = (f32[3,8,128]{2,1,0:T(8,128)S(1)}, f32[3,8,128]{2,1,0:T(8,128)S(1)}, u32[]{:S(2)}, u32[]{:S(2)}) collective-permute-start(f32[3,8,128]{2,1,0:T(8,128)S(1)} %get-tuple-element.37), channel_id=1, source_target_pairs={{0,8},{8,16},{16,24},{24,0},{1,9},{9,17},{17,25},{25,1},{2,10},{10... | collective-permute-start | bytes 36872 | tf_op jit(solution)/shard_map/ppermute | solution.py:528
  18.5 12.9 %collective-permute-start.4 = (f32[3,24,128]{2,1,0:T(8,128)S(1)}, f32[3,24,128]{2,1,0:T(8,128)S(1)}, u32[]{:S(2)}, u32[]{:S(2)}) collective-permute-start(f32[3,24,128]{2,1,0:T(8,128)S(1)} %get-tuple-element.38), channel_id=1, source_target_pairs={{0,1},{1,2},{2,3},{3,4},{4,5},{5,6},{6,7},{7,0},{8,9},{9,10},{10,1... | collective-permute-start | bytes 110600 | tf_op jit(solution)/shard_map/ppermute | solution.py:529
  18.8 12.6 %copy-start.2 = (f32[3,24,8,128]{3,2,1,0:T(8,128)S(1)}, f32[3,24,8,128]{3,2,1,0:T(8,128)}, u32[]{:S(2)}) copy-start(f32[3,24,8,128]{3,2,1,0:T(8,128)} %velocity_ref.1) | copy-start | bytes 884740
  18.8 12.6 %copy-start.3 = (f32[3,24,8,128]{3,2,1,0:T(8,128)S(1)}, f32[3,24,8,128]{3,2,1,0:T(8,128)}, u32[]{:S(2)}) copy-start(f32[3,24,8,128]{3,2,1,0:T(8,128)} %external_ref.1) | copy-start | bytes 884740
  18.8 12.6 %copy-start.4 = (f32[24,8,128]{2,1,0:T(8,128)S(1)}, f32[24,8,128]{2,1,0:T(8,128)}, u32[]{:S(2)}) copy-start(f32[24,8,128]{2,1,0:T(8,128)} %mass_ref.1) | copy-start | bytes 294916

commit v3 on v2

--- a/solution.py
+++ b/solution.py
@@ -205,37 +205,38 @@
             rows += [high, strain - high, high, jnp.zeros_like(high)]
         rows = jnp.concatenate(rows, axis=0).T
         strain_parts += [jnp.where(place == g, rows, 0.0).astype(BF16) for g in range(each)]
-    start = []
-    for c in range(0, number, part):
+    new_states, stresses = [None] * number, [None] * number
+
+    def chunk(c):
         high, low = split(jnp.concatenate(turned[c : c + part], axis=0))
         strain = jnp.concatenate(strain_parts[c : c + part], axis=0)
-        start.append(
-            dot(jnp.concatenate([high, low], axis=1), start0)
-            + dot(jnp.concatenate([high, strain], axis=1), start1)
-        )
-    now = start
-    for step in range(ITERS - 1):
-        later = []
-        for u in now:
+        start = dot(jnp.concatenate([high, low], axis=1), start0)
+        start = start + dot(jnp.concatenate([high, strain], axis=1), start1)
+        u = start
+        yield
+        for step in range(ITERS - 1):
             high, low = split(respond(u))
-            later.append(u - (dot(high, newton_high) + dot(low, newton_high) + dot(high, newton_low)))
-        now = later
-    last, moved = [], []
-    for first, u in zip(start, now):
+            u = u - (dot(high, newton_high) + dot(low, newton_high) + dot(high, newton_low))
+            yield
         h = respond(u)
-        last.append(u - dot(h.astype(BF16), newton_high))
-        moved.append(split(first - u + h))
-    new_states, stresses = [], []
-    for c, (high, low) in enumerate(moved):
+        last = u - dot(h.astype(BF16), newton_high)
+        high, low = split(start - u + h)
         both = dot(high, back)
         change = both[:, 0:count] + both[:, count:] + dot(low, back[:, 0:count])
+        yield
+        stress = lax.dot_general(
+            stress_m, respond(last).astype(BF16), (((1,), (1,)), ((), ())), preferred_element_type=F32
+        )
         for g in range(part):
-            new_states.append(states[c * part + g] - change[g * layers : (g + 1) * layers].T)
-    for u in last:
-        stress = lax.dot_general(
-            stress_m, respond(u).astype(BF16), (((1,), (1,)), ((), ())), preferred_element_type=F32
-        )
-        stresses += [stress[0:8, g * layers : (g + 1) * layers] for g in range(part)]
+            rows = slice(g * layers, (g + 1) * layers)
+            new_states[c + g] = states[c + g] - change[rows].T
+            stresses[c + g] = stress[0:8, rows]
+        yield
+
+    chunks = [chunk(c) for c in range(0, number, part)]
+    for stage in range(ITERS + 2):
+        for c in chunks:
+            next(c)
     return new_states, stresses
 
 
@@ -442,26 +443,31 @@
 
 def update_kernel(
     disp_ref, velocity_ref, external_ref, mass_ref, force_ref, xface_ref, yface_ref, cface_ref,
-    disp_out, velocity_out,
+    disp_hbm, velocity_hbm, disp_out, velocity_out, sems,
 ):
     rows, columns, layers = mass_ref.shape
+    tile = (columns, layers)
     less_x = lax.axis_index("gx") > 0
-    first_sub = lax.broadcasted_iota(jnp.int32, (columns, layers), 0) == 0
+    first_sub = lax.broadcasted_iota(jnp.int32, tile, 0) == 0
     first_sub = jnp.logical_and(first_sub, lax.axis_index("gy") > 0)
-    for i in range(rows):
-        factor = STEP / mass_ref[i]
-        for c in range(3):
+    factors = [STEP / mass_ref[i] for i in range(rows)]
+    copies = []
+    for c in range(3):
+        for i in range(rows):
             edge = yface_ref[c, i : i + 1]
             if i == 0:
                 edge = edge + jnp.where(less_x, cface_ref[c : c + 1], 0.0)
-            internal = force_ref[c, i] + jnp.where(
-                first_sub, jnp.broadcast_to(edge, (columns, layers)), 0.0
-            )
+            internal = force_ref[c, i] + jnp.where(first_sub, jnp.broadcast_to(edge, tile), 0.0)
             if i == 0:
                 internal = internal + jnp.where(less_x, xface_ref[c], 0.0)
-            velocity = velocity_ref[c, i] + factor * (external_ref[c, i] - internal)
+            velocity = velocity_ref[c, i] + factors[i] * (external_ref[c, i] - internal)
             velocity_out[c, i] = velocity
             disp_out[c, i] = disp_ref[c, i] + STEP * velocity
+        for n, (ours, whole) in enumerate(((velocity_out, velocity_hbm), (disp_out, disp_hbm))):
+            copies.append(pltpu.make_async_copy(ours.at[c], whole.at[c], sems.at[n, c]))
+            copies[-1].start()
+    for copy in copies:
+        copy.wait()
 
 
 def shape(*dims, dtype=F32):
@@ -547,7 +553,8 @@
         update_kernel,
         out_shape=(shape(3, rows, columns, layers),) * 2,
         in_specs=[VMEM] * 8,
-        out_specs=(VMEM,) * 2,
+        out_specs=(HBM,) * 2,
+        scratch_shapes=[pltpu.VMEM(displacement.shape, F32)] * 2 + [pltpu.SemaphoreType.DMA((2, 3))],
         compiler_params=pltpu.CompilerParams(vmem_limit_bytes=16 * 2**20),
     )(displacement, velocity, external_force, node_mass, force, xface, yface, cface)
     return displacement_next, velocity_next, new_state.reshape(micro_state.shape)

time: 31.9 us -> 31.1 us (0.975)
  the two profiles are of different devices: /device:TPU:1 before, /device:TPU:4 now
where the time goes in v3:
time: 31.1 us; the launch traced here: 30.7 us
  Pallas kernels  20.9 us (67%)
  starting transfers between devices  7.96 us (26%)
  local copies, waits for them, and re-layouts  1.01 us (3%)
  between operations  0.84 us (3%)
    pallas_call x1, Pallas kernels, on_device(): pl.pallas_call(functools.partial(inner_kernel, rows, columns), out_shape=...  12.3 us
    pallas_call x1, Pallas kernels, on_device(): pl.pallas_call(functools.partial(matrices_kernel, rows, columns), out_sha...  4.54 us
    ppermute x1, starting transfers between devices, on_device(): corner = lax.ppermute(corner, ('gx', 'gy'), both)  3.96 us
    pallas_call x1, Pallas kernels, on_device(): pl.pallas_call(functools.partial(edge_kernel, group, most), out_shape=(sh...  3.08 us
    ppermute x1, starting transfers between devices, on_device(): xface = lax.ppermute(xface, 'gx', back(along_x))  1.86 us
    unnamed x26, local copies, waits for them, and re-layouts  1.01 us
    pallas_call x1, Pallas kernels, on_device(): pl.pallas_call(update_kernel, out_shape=(shape(3, rows, columns, layers),...  0.91 us
    ppermute x1, starting transfers between devices, on_device(): xhalo = lax.ppermute(xhalo, 'gx', along_x)  0.84 us
  transfers between devices with their start and end apart: 6, of which 0 were waited for; matrix products, arithmetic and copies ran while one was open for 0% of the time, Pallas kernels for 55%

profile of v3, /device:TPU:4, one launch (start us, length us, event | category | flops | bytes accessed | tf_op | source)
XLA Modules:
  0.0 30.7 jit_solution(7839053542864327385)
XLA Ops:
  0.6 0.0 copy-start
  0.6 1.0 %copy-done = f32[3,24,8,128]{3,2,1,0:T(8,128)S(1)} copy-done((f32[3,24,8,128]{3,2,1,0:T(8,128)S(1)}, f32[3,24,8,128]{3,2,1,0:T(8,128)}, u32[]{:S(2)}) %copy-start) | copy-done | bytes 294936
  1.6 0.0 copy-start.6
  1.6 0.0 copy-start.8
  1.6 0.0 copy-start.9
  1.6 0.0 copy-start.10
  1.6 0.0 copy-start.11
  1.6 0.0 copy-start.12
  1.7 4.0 %collective-permute-start.2 = (f32[3,128]{1,0:T(4,128)S(1)}, f32[3,128]{1,0:T(4,128)S(1)}, u32[]{:S(2)}, u32[]{:S(2)}) collective-permute-start(f32[3,128]{1,0:T(4,128)S(1)} %get-tuple-element.26), channel_id=1, source_target_pairs={{9,0},{10,1},{11,2},{12,3},{13,4},{14,5},{15,6},{8,7},{17,8},{18,9... | collective-permute-start | bytes 4616 | tf_op jit(solution)/shard_map/ppermute | solution.py:500
  5.6 0.8 %collective-permute-start = (f32[3,8,128]{2,1,0:T(8,128)S(1)}, f32[3,8,128]{2,1,0:T(8,128)S(1)}, u32[]{:S(2)}, u32[]{:S(2)}) collective-permute-start(f32[3,8,128]{2,1,0:T(8,128)S(1)} %get-tuple-element.24), channel_id=1, source_target_pairs={{8,0},{16,8},{24,16},{0,24},{9,1},{17,9},{25,17},{1,25},{10,2},{18... | collective-permute-start | bytes 36872 | tf_op jit(solution)/shard_map/ppermute | solution.py:498
  6.5 0.5 %collective-permute-start.1 = (f32[3,24,128]{2,1,0:T(8,128)S(1)}, f32[3,24,128]{2,1,0:T(8,128)S(1)}, u32[]{:S(2)}, u32[]{:S(2)}) collective-permute-start(f32[3,24,128]{2,1,0:T(8,128)S(1)} %get-tuple-element.25), channel_id=1, source_target_pairs={{1,0},{2,1},{3,2},{4,3},{5,4},{6,5},{7,6},{0,7},{9,8},{10,9},{11,1... | collective-permute-start | bytes 110600 | tf_op jit(solution)/shard_map/ppermute | solution.py:499
  7.0 0.0 copy-done.6
  7.0 0.0 copy-done.8
  7.0 0.0 copy-done.9
  7.0 0.0 copy-done.10
  7.0 0.0 copy-done.11
  7.0 0.0 copy-done.12
  7.0 0.0 copy-start.1
  7.1 0.0 copy-start.5
  7.1 0.0 copy-start.7
  7.1 4.5 %shard_map.139 = (bf16[256,256]{1,0:T(8,128)(2,1)S(1)}, bf16[256,256]{1,0:T(8,128)(2,1)S(1)}, bf16[256,256]{1,0:T(8,128)(2,1)S(1)}, bf16[256,256]{1,0:T(8,128)(2...) custom-call(f32[256,128]{1,0:T(8,128)S(1)} %copy-done.6, ...), custom_call_target="tpu_custom_call" | custom-call | flops 10000000000 | bytes 1000000 | tf_op jit(solution)/shard_map/pallas_call | solution.py:503
  11.6 0.0 collective-permute-done.2.corner_ref
  11.6 0.0 collective-permute-done.xhalo_ref
  11.6 0.0 collective-permute-done.1.yhalo_ref
  11.7 0.0 copy-done.1
  11.7 0.0 copy-done.5
  11.7 0.0 copy-done.7
  11.7 3.1 %shard_map.141 = (f32[3,8,128]{2,1,0:T(8,128)S(1)}, f32[3,24,128]{2,1,0:T(8,128)S(1)}, f32[3,128]{1,0:T(4,128)S(1)}, f32[1536,128]{1,0:T(8,128)S(1)}, f32[1544,128]{1,0:T(8,128)S(1)}, /*index=5*/f32[6144,128]{1,0:T(8,128)S(1)}) custom-call(s32[8,128]{1,0:T(8,128)S(1)} %get-tuple-element.23.order_vmem, f32[3,24,8,128]{3,2,1,0:T(8,128)S(1)} %copy-done.1, ...), custom_call_target="tpu_custom_call" | custom-call | flops 10000000000 | bytes 10000000 | tf_op jit(solution)/shard_map/pallas_call | solution.py:521
  14.8 0.8 %collective-permute-start.5 = (f32[3,128]{1,0:T(4,128)S(1)}, f32[3,128]{1,0:T(4,128)S(1)}, u32[]{:S(2)}, u32[]{:S(2)}) collective-permute-start(f32[3,128]{1,0:T(4,128)S(1)} %get-tuple-element.39), channel_id=1, source_target_pairs={{0,9},{1,10},{2,11},{3,12},{4,13},{5,14},{6,15},{7,8},{8,17},{9,18... | collective-permute-start | bytes 4616 | tf_op jit(solution)/shard_map/ppermute | solution.py:536
  15.5 1.9 %collective-permute-start.3 = (f32[3,8,128]{2,1,0:T(8,128)S(1)}, f32[3,8,128]{2,1,0:T(8,128)S(1)}, u32[]{:S(2)}, u32[]{:S(2)}) collective-permute-start(f32[3,8,128]{2,1,0:T(8,128)S(1)} %get-tuple-element.37), channel_id=1, source_target_pairs={{0,8},{8,16},{16,24},{24,0},{1,9},{9,17},{17,25},{25,1},{2,10},{10... | collective-permute-start | bytes 36872 | tf_op jit(solution)/shard_map/ppermute | solution.py:534
  17.4 0.0 collective-permute-start.4
  17.4 0.0 copy-start.2
  17.4 0.0 copy-start.3
  17.4 0.0 copy-start.4
  17.4 12.3 %shard_map.142 = (f32[3,24,8,128]{3,2,1,0:T(8,128)S(1)}, f32[128,48,128]{2,1,0:T(8,128)}) custom-call(s32[8,128]{1,0:T(8,128)S(1)} %get-tuple-element.23.order_vmem, f32[6144,128]{1,0:T(8,128)S(1)} %bitcast.8, f32[1536,128]{1,0:T(8,128)S(1)} %get-tuple-element.33.strain_ref, f32[1544,128]{1,0:T(8,128)S(1)} %get-tuple-element.34.stress_in, ...), custom_call_target="tpu_custom_call" | custom-call | flops 20000000000 | bytes 10000000 | tf_op jit(solution)/shard_map/pallas_call | solution.py:538
  29.7 0.0 collective-permute-done.5.cface_ref
  29.7 0.0 collective-permute-done.3.xface_ref
  29.7 0.0 collective-permute-done.4.yface_ref
  29.7 0.0 copy-done.2
  29.8 0.0 copy-done.3
  29.8 0.0 copy-done.4
  29.8 0.9 %shard_map.143 = (f32[3,24,8,128]{3,2,1,0:T(8,128)}, f32[3,24,8,128]{3,2,1,0:T(8,128)}) custom-call(f32[3,24,8,128]{3,2,1,0:T(8,128)S(1)} %copy-done.1, f32[3,24,8,128]{3,2,1,0:T(8,128)S(1)} %copy-done.2, f32[3,24,8,128]{3,2,1,0:T(8,128)S(1)} %copy-done.3, f32[24,8,128]{2,1,0:T(8,128)S(1)} %copy-done.4, f32[3,24,8,128]{3,2,1,0:T(8,128)S(1)} %get-tuple-element.36.force_ref, ...), custom_call_target="tpu_custom_call" | custom-call | tf_op jit(solution)/shard_map/pallas_call | solution.py:552
  (1 shorter events, 0.0 us)
Async XLA Ops:
  0.6 1.0 %copy-start = (f32[3,24,8,128]{3,2,1,0:T(8,128)S(1)}, f32[3,24,8,128]{3,2,1,0:T(8,128)}, u32[]{:S(2)}) copy-start(f32[3,24,8,128]{3,2,1,0:T(8,128)} %disp_ref.5) | copy-start | bytes 884740
  1.6 5.4 %copy-start.6 = (f32[256,128]{1,0:T(8,128)S(1)}, f32[256,128]{1,0:T(8,128)}, u32[]{:S(2)}) copy-start(f32[256,128]{1,0:T(8,128)} %modes_ref.1) | copy-start | bytes 393220
  1.6 5.4 %copy-start.8 = (f32[256,6]{0,1:T(8,128)S(1)}, f32[256,6]{0,1:T(8,128)}, u32[]{:S(2)}) copy-start(f32[256,6]{0,1:T(8,128)} %param.19) | copy-start | bytes 18436
  1.6 5.4 %copy-start.9 = (s32[1,8,48]{2,1,0:T(8,128)S(1)}, s32[1,8,48]{2,1,0:T(8,128)}, u32[]{:S(2)}) copy-start(s32[1,8,48]{2,1,0:T(8,128)} %param.17) | copy-start | bytes 4612
  1.6 5.4 %copy-start.10 = (f32[256]{0:T(256)S(1)}, f32[256]{0:T(256)}, u32[]{:S(2)}) copy-start(f32[256]{0:T(256)} %param.21) | copy-start | bytes 3076
  1.6 5.4 %copy-start.11 = (f32[256]{0:T(256)S(1)}, f32[256]{0:T(256)}, u32[]{:S(2)}) copy-start(f32[256]{0:T(256)} %param.22) | copy-start | bytes 3076
  1.6 5.4 %copy-start.12 = (f32[256]{0:T(256)S(1)}, f32[256]{0:T(256)}, u32[]{:S(2)}) copy-start(f32[256]{0:T(256)} %param.23) | copy-start | bytes 3076
  1.7 10.0 %collective-permute-start.2 = (f32[3,128]{1,0:T(4,128)S(1)}, f32[3,128]{1,0:T(4,128)S(1)}, u32[]{:S(2)}, u32[]{:S(2)}) collective-permute-start(f32[3,128]{1,0:T(4,128)S(1)} %get-tuple-element.26), channel_id=1, source_target_pairs={{9,0},{10,1},{11,2},{12,3},{13,4},{14,5},{15,6},{8,7},{17,8},{18,9... | collective-permute-start | bytes 4616 | tf_op jit(solution)/shard_map/ppermute | solution.py:500
  5.6 6.0 %collective-permute-start = (f32[3,8,128]{2,1,0:T(8,128)S(1)}, f32[3,8,128]{2,1,0:T(8,128)S(1)}, u32[]{:S(2)}, u32[]{:S(2)}) collective-permute-start(f32[3,8,128]{2,1,0:T(8,128)S(1)} %get-tuple-element.24), channel_id=1, source_target_pairs={{8,0},{16,8},{24,16},{0,24},{9,1},{17,9},{25,17},{1,25},{10,2},{18... | collective-permute-start | bytes 36872 | tf_op jit(solution)/shard_map/ppermute | solution.py:498
  6.5 5.2 %collective-permute-start.1 = (f32[3,24,128]{2,1,0:T(8,128)S(1)}, f32[3,24,128]{2,1,0:T(8,128)S(1)}, u32[]{:S(2)}, u32[]{:S(2)}) collective-permute-start(f32[3,24,128]{2,1,0:T(8,128)S(1)} %get-tuple-element.25), channel_id=1, source_target_pairs={{1,0},{2,1},{3,2},{4,3},{5,4},{6,5},{7,6},{0,7},{9,8},{10,9},{11,1... | collective-permute-start | bytes 110600 | tf_op jit(solution)/shard_map/ppermute | solution.py:499
  7.0 4.6 %copy-start.1 = (f32[3,24,8,128]{3,2,1,0:T(8,128)S(1)}, f32[3,24,8,128]{3,2,1,0:T(8,128)}, u32[]{:S(2)}) copy-start(f32[3,24,8,128]{3,2,1,0:T(8,128)} %disp_ref.5) | copy-start | bytes 884740
  7.1 4.6 %copy-start.5 = (f32[1,1,128,48,128]{4,3,2,1,0:T(8,128)S(1)}, f32[1,1,128,48,128]{4,3,2,1,0:T(8,128)}, u32[]{:S(2)}) copy-start(f32[1,1,128,48,128]{4,3,2,1,0:T(8,128)} %param.18) | copy-start | bytes 9437188
  7.1 4.6 %copy-start.7 = (f32[24,8,128]{2,1,0:T(8,128)S(1)}, f32[24,8,128]{2,1,0:T(8,128)}, u32[]{:S(2)}) copy-start(f32[24,8,128]{2,1,0:T(8,128)} %stiff_ref.1) | copy-start | bytes 294916
  14.8 14.9 %collective-permute-start.5 = (f32[3,128]{1,0:T(4,128)S(1)}, f32[3,128]{1,0:T(4,128)S(1)}, u32[]{:S(2)}, u32[]{:S(2)}) collective-permute-start(f32[3,128]{1,0:T(4,128)S(1)} %get-tuple-element.39), channel_id=1, source_target_pairs={{0,9},{1,10},{2,11},{3,12},{4,13},{5,14},{6,15},{7,8},{8,17},{9,18... | collective-permute-start | bytes 4616 | tf_op jit(solution)/shard_map/ppermute | solution.py:536
  15.5 14.2 %collective-permute-start.3 = (f32[3,8,128]{2,1,0:T(8,128)S(1)}, f32[3,8,128]{2,1,0:T(8,128)S(1)}, u32[]{:S(2)}, u32[]{:S(2)}) collective-permute-start(f32[3,8,128]{2,1,0:T(8,128)S(1)} %get-tuple-element.37), channel_id=1, source_target_pairs={{0,8},{8,16},{16,24},{24,0},{1,9},{9,17},{17,25},{25,1},{2,10},{10... | collective-permute-start | bytes 36872 | tf_op jit(solution)/shard_map/ppermute | solution.py:534
  17.4 12.4 %collective-permute-start.4 = (f32[3,24,128]{2,1,0:T(8,128)S(1)}, f32[3,24,128]{2,1,0:T(8,128)S(1)}, u32[]{:S(2)}, u32[]{:S(2)}) collective-permute-start(f32[3,24,128]{2,1,0:T(8,128)S(1)} %get-tuple-element.38), channel_id=1, source_target_pairs={{0,1},{1,2},{2,3},{3,4},{4,5},{5,6},{6,7},{7,0},{8,9},{9,10},{10,1... | collective-permute-start | bytes 110600 | tf_op jit(solution)/shard_map/ppermute | solution.py:535
  17.4 12.4 %copy-start.2 = (f32[3,24,8,128]{3,2,1,0:T(8,128)S(1)}, f32[3,24,8,128]{3,2,1,0:T(8,128)}, u32[]{:S(2)}) copy-start(f32[3,24,8,128]{3,2,1,0:T(8,128)} %velocity_ref.1) | copy-start | bytes 884740
  17.4 12.4 %copy-start.3 = (f32[3,24,8,128]{3,2,1,0:T(8,128)S(1)}, f32[3,24,8,128]{3,2,1,0:T(8,128)}, u32[]{:S(2)}) copy-start(f32[3,24,8,128]{3,2,1,0:T(8,128)} %external_ref.1) | copy-start | bytes 884740
  17.4 12.4 %copy-start.4 = (f32[24,8,128]{2,1,0:T(8,128)S(1)}, f32[24,8,128]{2,1,0:T(8,128)}, u32[]{:S(2)}) copy-start(f32[24,8,128]{2,1,0:T(8,128)} %mass_ref.1) | copy-start | bytes 294916
